TPU v7x, 128 devices: a whole 4x4x4 slice. The times are simulated.
128 devices in a mesh: blk: 64 (over z, y, x), band: 2 (over core).
Axes of the slice: x: 4, y: 4, z: 4, core: 2. Of those that a mesh axis runs over, the one named last changes fastest.
Arguments:
- traces: bfloat16 [4096, 2, 8192], P('blk', None, 'band'), may hold values from -80 to 80
- sources: bfloat16 [128, 2, 8192], P('blk', None, 'band'), may hold values from -80 to 80
- owner: int32 [4096, 1], P('blk'), may hold values from 0 to 63; in each aligned block of 64 rows (0 to 63, 64 to 127, ...) at most 2 rows name the same one
Outputs:
- gathers: float32 [128, 16, 128, 256], P('blk', None, 'band')
Inputs may be any that keep to these rules, and one draw needn't show every extreme that they name: Among the 64 stations of one device's rows, at most 2 name the same owner block, and some owner block is named by exactly 2 of them in every draw.
All inputs are finite; a program needn't handle non-finite values.
Results may differ from a plain program's by a relative error of at most 0.017.
Values may be sent and summed in bfloat16 or wider, within the bound.
A program may use at most 128 MiB of HBM per device.

v0:
```python
import math

import jax
import jax.numpy as jnp
from jax import lax
from jax.sharding import PartitionSpec as P

BINS = 8192
LAGS = 2048
DEC = 8


EPS = 1e-06


def from_behind(block, axis, distance):
    devices = range(lax.axis_size(axis))
    route = [((i - distance) % len(devices), i) for i in devices]
    return lax.ppermute(block, axis, route)


def per_device(traces, sources, owner):
    blocks = lax.axis_size("blk")
    band_count = lax.axis_size("band")
    station_count = traces.shape[0]
    source_count = sources.shape[0]
    group_bins = traces.shape[2]
    capacity = max(2, 2 * station_count // blocks)
    slot_total = blocks * capacity
    slot_share = slot_total // band_count
    lags_out = LAGS // DEC
    cycle_steps = blocks // 4
    trace_float = traces.astype(jnp.float32)
    source_float = sources.astype(jnp.float32)
    trace_power, source_power = lax.psum(
        (
            jnp.sum(trace_float * trace_float, axis=(1, 2)),
            jnp.sum(source_float * source_float, axis=(1, 2)),
        ),
        "band",
    )
    white_traces = (
        (trace_float * lax.rsqrt(trace_power / (2 * BINS) + EPS)[:, None, None])
        .astype(jnp.bfloat16)
        .reshape(station_count, 2 * group_bins)
    )
    white_sources = (
        (source_float * lax.rsqrt(source_power / (2 * BINS) + EPS)[:, None, None])
        .astype(jnp.bfloat16)
        .reshape(source_count, 2 * group_bins)
    )
    owners = owner[:, 0]
    owner_hits = (owners[:, None] == jnp.arange(blocks, dtype=jnp.int32)[None, :]).astype(jnp.int32)
    earlier = jnp.cumsum(owner_hits, axis=0) - owner_hits
    arrival = jnp.sum(owner_hits * earlier, axis=1)
    slot_index = owners * capacity + arrival
    placing = (jnp.arange(slot_total, dtype=jnp.int32)[:, None] == slot_index[None, :]).astype(
        jnp.bfloat16
    )
    outgoing = jnp.dot(placing, white_traces, preferred_element_type=jnp.float32).astype(
        jnp.bfloat16
    )
    outgoing = outgoing.reshape(blocks, capacity, 2 * group_bins)
    resident = lax.all_to_all(outgoing, "blk", split_axis=0, concat_axis=0, tiled=True).reshape(
        slot_total, 2 * group_bins
    )
    bin_index = lax.axis_index("band") * group_bins + jnp.arange(group_bins, dtype=jnp.int32)
    lag_value = (jnp.arange(lags_out, dtype=jnp.int32) - lags_out // 2) * DEC
    phase_angle = jnp.mod(bin_index[:, None] * lag_value[None, :], BINS).astype(jnp.float32) * (
        2.0 * math.pi / BINS
    )
    cosine_table = jnp.cos(phase_angle)[:, None, :]
    sine_table = jnp.sin(phase_angle)[:, None, :]
    norm_scale = BINS ** (-0.5)

    def correlate(receivers, kernel):
        return lax.psum_scatter(
            jnp.dot(receivers, kernel, preferred_element_type=jnp.float32).astype(jnp.bfloat16),
            "band",
            scatter_dimension=0,
            tiled=True,
        ).astype(jnp.float32)

    source_values = white_sources.astype(jnp.float32)
    real_part = source_values[:, :group_bins].T[:, :, None]
    imag_part = source_values[:, group_bins:].T[:, :, None]
    kernel_real = real_part * cosine_table + imag_part * sine_table
    kernel_imag = imag_part * cosine_table - real_part * sine_table
    joined = jnp.concatenate([kernel_real, kernel_imag], axis=0) * norm_scale
    kernel = joined.reshape(2 * group_bins, source_count * lags_out).astype(jnp.bfloat16)

    def advance(visiting, unused):
        partial_value = correlate(visiting, kernel)
        return (from_behind(visiting, "blk", 1), partial_value)

    visiting, partials = lax.scan(advance, resident, None, length=cycle_steps - 1)
    partials = jnp.concatenate([partials, correlate(visiting, kernel)[None]], axis=0)
    partials = partials.reshape(cycle_steps, slot_share, source_count, lags_out)
    return jnp.transpose(partials, (2, 0, 1, 3))


def solution(mesh):
    placed = (P("blk", None, "band"), P("blk", None, "band"), P("blk", None))
    return jax.shard_map(
        per_device,
        mesh=mesh,
        in_specs=placed,
        out_specs=P("blk", None, "band", None),
        check_vma=False,
    )
```

profile of v0, /device:TPU:1, one launch (start us, length us, event | category | flops | bytes accessed | tf_op | source)
XLA Modules:
  0.0 849.4 jit_solution(12781767650831001594)
XLA Ops:
  38.0 16.4 %fusion.7 = (f32[4096,256]{1,0:T(8,128)S(1)}, f32[4096,256]{1,0:T(8,128)S(1)}) fusion(s32[256]{0:T(256)S(1)} %add_multiply_fusion, s32[4096]{0:T(1024)S(1)} %iota_add_fusion), kind=kLoop, calls=%fused_computation.21 | loop fusion | flops 14680064 | bytes 8406016 | tf_op jit(solution)/shard_map/cos | solution.py:72
  54.4 22.5 %multiply_add_fusion = (f32[4096,2,256]{2,1,0:T(2,128)}, f32[4096,2,256]{2,1,0:T(2,128)}) fusion(f32[4096,256]{1,0:T(8,128)S(1)} %get-tuple-element.45, f32[4096,2]{1,0:T(8,128)S(1)} %copy-done, f32[4096,256]{1,0:T(8,128)S(1)} %get-tuple-element.44, f32[4096,2]{1,0:T(8,128)S(1)} %copy.7), kind=kLoop, calls=%fused_computation.6 | loop fusion | flops 12582912 | bytes 25231360 | tf_op jit(solution)/shard_map/add | solution.py:87
  98.7 716.1 %while.12 = (s32[]{:T(128)}, bf16[128,8192]{1,0:T(8,128)(2,1)}, f32[15,64,512]{2,1,0:T(8,128)}, bf16[8192,512]{1,0:T(8,128)(2,1)}, s32[]{:T(128)}) while((s32[]{:T(128)}, bf16[128,8192]{1,0:T(8,128)(2,1)}, f32[15,64,512]{2,1,0:T(8,128)}, bf16[8192,512]{1,0:T(8,128)(2,1)}, s32[]{:T(128)}) %tuple.21), condition=%wide.region_8.9_spmd, body=%wide.region_6.8_spmd.sunk | while | flops 1073840128 | bytes 23986328 | solution.py:96
  106.4 12.2 %reduce-scatter.5.cloned.1.call-done = bf16[64,512]{1,0:T(8,128)(2,1)} async-done(((bf16[128,512]{1,0:T(8,128)(2,1)}), bf16[64,512]{1,0:T(8,128)(2,1)}) %reduce-scatter.5.cloned.1.call-update) | async-done | bytes 65552 | tf_op jit(solution)/shard_map/while/body/eval_jaxpr/reduce_scatter | solution.py:77
  120.1 32.3 %collective-permute-done = bf16[128,8192]{1,0:T(8,128)(2,1)} collective-permute-done((bf16[128,8192]{1,0:T(8,128)(2,1)S(1)}, bf16[128,8192]{1,0:T(8,128)(2,1)}, u32[]{:S(2)}, u32[]{:S(2)}) %collective-permute-start) | collective-permute-done | bytes 2097184 | tf_op jit(solution)/shard_map/while/body/eval_jaxpr/ppermute | solution.py:19
  159.3 12.3 %reduce-scatter.5.cloned.1.call-done = bf16[64,512]{1,0:T(8,128)(2,1)} async-done(((bf16[128,512]{1,0:T(8,128)(2,1)}), bf16[64,512]{1,0:T(8,128)(2,1)}) %reduce-scatter.5.cloned.1.call-update) | async-done | bytes 65552 | tf_op jit(solution)/shard_map/while/body/eval_jaxpr/reduce_scatter | solution.py:77
  173.2 32.0 %collective-permute-done = bf16[128,8192]{1,0:T(8,128)(2,1)} collective-permute-done((bf16[128,8192]{1,0:T(8,128)(2,1)S(1)}, bf16[128,8192]{1,0:T(8,128)(2,1)}, u32[]{:S(2)}, u32[]{:S(2)}) %collective-permute-start) | collective-permute-done | bytes 2097184 | tf_op jit(solution)/shard_map/while/body/eval_jaxpr/ppermute | solution.py:19
  212.1 13.2 %reduce-scatter.5.cloned.1.call-done = bf16[64,512]{1,0:T(8,128)(2,1)} async-done(((bf16[128,512]{1,0:T(8,128)(2,1)}), bf16[64,512]{1,0:T(8,128)(2,1)}) %reduce-scatter.5.cloned.1.call-update) | async-done | bytes 65552 | tf_op jit(solution)/shard_map/while/body/eval_jaxpr/reduce_scatter | solution.py:77
  226.8 30.2 %collective-permute-done = bf16[128,8192]{1,0:T(8,128)(2,1)} collective-permute-done((bf16[128,8192]{1,0:T(8,128)(2,1)S(1)}, bf16[128,8192]{1,0:T(8,128)(2,1)}, u32[]{:S(2)}, u32[]{:S(2)}) %collective-permute-start) | collective-permute-done | bytes 2097184 | tf_op jit(solution)/shard_map/while/body/eval_jaxpr/ppermute | solution.py:19
  263.9 14.2 %reduce-scatter.5.cloned.1.call-done = bf16[64,512]{1,0:T(8,128)(2,1)} async-done(((bf16[128,512]{1,0:T(8,128)(2,1)}), bf16[64,512]{1,0:T(8,128)(2,1)}) %reduce-scatter.5.cloned.1.call-update) | async-done | bytes 65552 | tf_op jit(solution)/shard_map/while/body/eval_jaxpr/reduce_scatter | solution.py:77
  279.6 28.3 %collective-permute-done = bf16[128,8192]{1,0:T(8,128)(2,1)} collective-permute-done((bf16[128,8192]{1,0:T(8,128)(2,1)S(1)}, bf16[128,8192]{1,0:T(8,128)(2,1)}, u32[]{:S(2)}, u32[]{:S(2)}) %collective-permute-start) | collective-permute-done | bytes 2097184 | tf_op jit(solution)/shard_map/while/body/eval_jaxpr/ppermute | solution.py:19
  314.8 15.1 %reduce-scatter.5.cloned.1.call-done = bf16[64,512]{1,0:T(8,128)(2,1)} async-done(((bf16[128,512]{1,0:T(8,128)(2,1)}), bf16[64,512]{1,0:T(8,128)(2,1)}) %reduce-scatter.5.cloned.1.call-update) | async-done | bytes 65552 | tf_op jit(solution)/shard_map/while/body/eval_jaxpr/reduce_scatter | solution.py:77
  331.4 26.5 %collective-permute-done = bf16[128,8192]{1,0:T(8,128)(2,1)} collective-permute-done((bf16[128,8192]{1,0:T(8,128)(2,1)S(1)}, bf16[128,8192]{1,0:T(8,128)(2,1)}, u32[]{:S(2)}, u32[]{:S(2)}) %collective-permute-start) | collective-permute-done | bytes 2097184 | tf_op jit(solution)/shard_map/while/body/eval_jaxpr/ppermute | solution.py:19
  364.8 16.0 %reduce-scatter.5.cloned.1.call-done = bf16[64,512]{1,0:T(8,128)(2,1)} async-done(((bf16[128,512]{1,0:T(8,128)(2,1)}), bf16[64,512]{1,0:T(8,128)(2,1)}) %reduce-scatter.5.cloned.1.call-update) | async-done | bytes 65552 | tf_op jit(solution)/shard_map/while/body/eval_jaxpr/reduce_scatter | solution.py:77
  382.3 24.6 %collective-permute-done = bf16[128,8192]{1,0:T(8,128)(2,1)} collective-permute-done((bf16[128,8192]{1,0:T(8,128)(2,1)S(1)}, bf16[128,8192]{1,0:T(8,128)(2,1)}, u32[]{:S(2)}, u32[]{:S(2)}) %collective-permute-start) | collective-permute-done | bytes 2097184 | tf_op jit(solution)/shard_map/while/body/eval_jaxpr/ppermute | solution.py:19
  413.9 16.9 %reduce-scatter.5.cloned.1.call-done = bf16[64,512]{1,0:T(8,128)(2,1)} async-done(((bf16[128,512]{1,0:T(8,128)(2,1)}), bf16[64,512]{1,0:T(8,128)(2,1)}) %reduce-scatter.5.cloned.1.call-update) | async-done | bytes 65552 | tf_op jit(solution)/shard_map/while/body/eval_jaxpr/reduce_scatter | solution.py:77
  432.3 22.8 %collective-permute-done = bf16[128,8192]{1,0:T(8,128)(2,1)} collective-permute-done((bf16[128,8192]{1,0:T(8,128)(2,1)S(1)}, bf16[128,8192]{1,0:T(8,128)(2,1)}, u32[]{:S(2)}, u32[]{:S(2)}) %collective-permute-start) | collective-permute-done | bytes 2097184 | tf_op jit(solution)/shard_map/while/body/eval_jaxpr/ppermute | solution.py:19
  462.0 17.9 %reduce-scatter.5.cloned.1.call-done = bf16[64,512]{1,0:T(8,128)(2,1)} async-done(((bf16[128,512]{1,0:T(8,128)(2,1)}), bf16[64,512]{1,0:T(8,128)(2,1)}) %reduce-scatter.5.cloned.1.call-update) | async-done | bytes 65552 | tf_op jit(solution)/shard_map/while/body/eval_jaxpr/reduce_scatter | solution.py:77
  481.4 21.0 %collective-permute-done = bf16[128,8192]{1,0:T(8,128)(2,1)} collective-permute-done((bf16[128,8192]{1,0:T(8,128)(2,1)S(1)}, bf16[128,8192]{1,0:T(8,128)(2,1)}, u32[]{:S(2)}, u32[]{:S(2)}) %collective-permute-start) | collective-permute-done | bytes 2097184 | tf_op jit(solution)/shard_map/while/body/eval_jaxpr/ppermute | solution.py:19
  509.3 18.8 %reduce-scatter.5.cloned.1.call-done = bf16[64,512]{1,0:T(8,128)(2,1)} async-done(((bf16[128,512]{1,0:T(8,128)(2,1)}), bf16[64,512]{1,0:T(8,128)(2,1)}) %reduce-scatter.5.cloned.1.call-update) | async-done | bytes 65552 | tf_op jit(solution)/shard_map/while/body/eval_jaxpr/reduce_scatter | solution.py:77
  529.5 19.1 %collective-permute-done = bf16[128,8192]{1,0:T(8,128)(2,1)} collective-permute-done((bf16[128,8192]{1,0:T(8,128)(2,1)S(1)}, bf16[128,8192]{1,0:T(8,128)(2,1)}, u32[]{:S(2)}, u32[]{:S(2)}) %collective-permute-start) | collective-permute-done | bytes 2097184 | tf_op jit(solution)/shard_map/while/body/eval_jaxpr/ppermute | solution.py:19
  555.6 19.7 %reduce-scatter.5.cloned.1.call-done = bf16[64,512]{1,0:T(8,128)(2,1)} async-done(((bf16[128,512]{1,0:T(8,128)(2,1)}), bf16[64,512]{1,0:T(8,128)(2,1)}) %reduce-scatter.5.cloned.1.call-update) | async-done | bytes 65552 | tf_op jit(solution)/shard_map/while/body/eval_jaxpr/reduce_scatter | solution.py:77
  576.8 17.3 %collective-permute-done = bf16[128,8192]{1,0:T(8,128)(2,1)} collective-permute-done((bf16[128,8192]{1,0:T(8,128)(2,1)S(1)}, bf16[128,8192]{1,0:T(8,128)(2,1)}, u32[]{:S(2)}, u32[]{:S(2)}) %collective-permute-start) | collective-permute-done | bytes 2097184 | tf_op jit(solution)/shard_map/while/body/eval_jaxpr/ppermute | solution.py:19
  601.0 20.6 %reduce-scatter.5.cloned.1.call-done = bf16[64,512]{1,0:T(8,128)(2,1)} async-done(((bf16[128,512]{1,0:T(8,128)(2,1)}), bf16[64,512]{1,0:T(8,128)(2,1)}) %reduce-scatter.5.cloned.1.call-update) | async-done | bytes 65552 | tf_op jit(solution)/shard_map/while/body/eval_jaxpr/reduce_scatter | solution.py:77
  623.1 15.4 %collective-permute-done = bf16[128,8192]{1,0:T(8,128)(2,1)} collective-permute-done((bf16[128,8192]{1,0:T(8,128)(2,1)S(1)}, bf16[128,8192]{1,0:T(8,128)(2,1)}, u32[]{:S(2)}, u32[]{:S(2)}) %collective-permute-start) | collective-permute-done | bytes 2097184 | tf_op jit(solution)/shard_map/while/body/eval_jaxpr/ppermute | solution.py:19
  645.4 22.0 %reduce-scatter.5.cloned.1.call-done = bf16[64,512]{1,0:T(8,128)(2,1)} async-done(((bf16[128,512]{1,0:T(8,128)(2,1)}), bf16[64,512]{1,0:T(8,128)(2,1)}) %reduce-scatter.5.cloned.1.call-update) | async-done | bytes 65552 | tf_op jit(solution)/shard_map/while/body/eval_jaxpr/reduce_scatter | solution.py:77
  668.9 13.7 %collective-permute-done = bf16[128,8192]{1,0:T(8,128)(2,1)} collective-permute-done((bf16[128,8192]{1,0:T(8,128)(2,1)S(1)}, bf16[128,8192]{1,0:T(8,128)(2,1)}, u32[]{:S(2)}, u32[]{:S(2)}) %collective-permute-start) | collective-permute-done | bytes 2097184 | tf_op jit(solution)/shard_map/while/body/eval_jaxpr/ppermute | solution.py:19
  689.5 23.7 %reduce-scatter.5.cloned.1.call-done = bf16[64,512]{1,0:T(8,128)(2,1)} async-done(((bf16[128,512]{1,0:T(8,128)(2,1)}), bf16[64,512]{1,0:T(8,128)(2,1)}) %reduce-scatter.5.cloned.1.call-update) | async-done | bytes 65552 | tf_op jit(solution)/shard_map/while/body/eval_jaxpr/reduce_scatter | solution.py:77
  714.7 12.0 %collective-permute-done = bf16[128,8192]{1,0:T(8,128)(2,1)} collective-permute-done((bf16[128,8192]{1,0:T(8,128)(2,1)S(1)}, bf16[128,8192]{1,0:T(8,128)(2,1)}, u32[]{:S(2)}, u32[]{:S(2)}) %collective-permute-start) | collective-permute-done | bytes 2097184 | tf_op jit(solution)/shard_map/while/body/eval_jaxpr/ppermute | solution.py:19
  733.6 25.4 %reduce-scatter.5.cloned.1.call-done = bf16[64,512]{1,0:T(8,128)(2,1)} async-done(((bf16[128,512]{1,0:T(8,128)(2,1)}), bf16[64,512]{1,0:T(8,128)(2,1)}) %reduce-scatter.5.cloned.1.call-update) | async-done | bytes 65552 | tf_op jit(solution)/shard_map/while/body/eval_jaxpr/reduce_scatter | solution.py:77
  777.7 27.1 %reduce-scatter.5.cloned.1.call-done = bf16[64,512]{1,0:T(8,128)(2,1)} async-done(((bf16[128,512]{1,0:T(8,128)(2,1)}), bf16[64,512]{1,0:T(8,128)(2,1)}) %reduce-scatter.5.cloned.1.call-update) | async-done | bytes 65552 | tf_op jit(solution)/shard_map/while/body/eval_jaxpr/reduce_scatter | solution.py:77
  823.3 15.0 %reduce-scatter.3.cloned.1.call-done = bf16[64,512]{1,0:T(8,128)(2,1)} async-done(((bf16[128,512]{1,0:T(8,128)(2,1)}), bf16[64,512]{1,0:T(8,128)(2,1)}) %reduce-scatter.3.cloned.1.call-update) | async-done | bytes 65552 | tf_op jit(solution)/shard_map/reduce_scatter | solution.py:77
  (135 shorter events, 210.4 us)
Async XLA Ops:
  23.4 71.2 %all-to-all-start = ((bf16[64,2,8192]{2,1,0:T(2,128)(2,1)}), bf16[64,2,8192]{2,1,0:T(2,128)(2,1)}, u32[]{:S(2)}, u32[]{:S(2)}) async-start(bf16[64,2,8192]{2,1,0:T(2,128)(2,1)} %reshape.116), calls=%async_computation.1 | async-start | bytes 4194304 | tf_op jit(solution)/shard_map/all_to_all | solution.py:64
  98.7 19.9 %reduce-scatter.5.cloned.1.call-start = ((), (), s32[]{:S(2)}) async-start(), calls=%async_computation.4 | async-start | bytes 196608 | tf_op jit(solution)/shard_map/while/body/eval_jaxpr/reduce_scatter | solution.py:77
  100.3 52.1 %collective-permute-start = (bf16[128,8192]{1,0:T(8,128)(2,1)S(1)}, bf16[128,8192]{1,0:T(8,128)(2,1)}, u32[]{:S(2)}, u32[]{:S(2)}) collective-permute-start(bf16[128,8192]{1,0:T(8,128)(2,1)S(1)} %copy.19), channel_id=1, source_target_pairs={{126,0},{0,2},{2,4},{4,6},{6,8},{8,10},{10,12},{12,14},{14,16},{16... | collective-permute-start | bytes 6291464 | tf_op jit(solution)/shard_map/while/body/eval_jaxpr/ppermute | solution.py:19
  152.4 19.3 %reduce-scatter.5.cloned.1.call-start = ((), (), s32[]{:S(2)}) async-start(), calls=%async_computation.4 | async-start | bytes 196608 | tf_op jit(solution)/shard_map/while/body/eval_jaxpr/reduce_scatter | solution.py:77
  154.0 51.2 %collective-permute-start = (bf16[128,8192]{1,0:T(8,128)(2,1)S(1)}, bf16[128,8192]{1,0:T(8,128)(2,1)}, u32[]{:S(2)}, u32[]{:S(2)}) collective-permute-start(bf16[128,8192]{1,0:T(8,128)(2,1)S(1)} %copy.19), channel_id=1, source_target_pairs={{126,0},{0,2},{2,4},{4,6},{6,8},{8,10},{10,12},{12,14},{14,16},{16... | collective-permute-start | bytes 6291464 | tf_op jit(solution)/shard_map/while/body/eval_jaxpr/ppermute | solution.py:19
  205.2 20.2 %reduce-scatter.5.cloned.1.call-start = ((), (), s32[]{:S(2)}) async-start(), calls=%async_computation.4 | async-start | bytes 196608 | tf_op jit(solution)/shard_map/while/body/eval_jaxpr/reduce_scatter | solution.py:77
  206.8 50.2 %collective-permute-start = (bf16[128,8192]{1,0:T(8,128)(2,1)S(1)}, bf16[128,8192]{1,0:T(8,128)(2,1)}, u32[]{:S(2)}, u32[]{:S(2)}) collective-permute-start(bf16[128,8192]{1,0:T(8,128)(2,1)S(1)} %copy.19), channel_id=1, source_target_pairs={{126,0},{0,2},{2,4},{4,6},{6,8},{8,10},{10,12},{12,14},{14,16},{16... | collective-permute-start | bytes 6291464 | tf_op jit(solution)/shard_map/while/body/eval_jaxpr/ppermute | solution.py:19
  257.0 21.1 %reduce-scatter.5.cloned.1.call-start = ((), (), s32[]{:S(2)}) async-start(), calls=%async_computation.4 | async-start | bytes 196608 | tf_op jit(solution)/shard_map/while/body/eval_jaxpr/reduce_scatter | solution.py:77
  258.6 49.3 %collective-permute-start = (bf16[128,8192]{1,0:T(8,128)(2,1)S(1)}, bf16[128,8192]{1,0:T(8,128)(2,1)}, u32[]{:S(2)}, u32[]{:S(2)}) collective-permute-start(bf16[128,8192]{1,0:T(8,128)(2,1)S(1)} %copy.19), channel_id=1, source_target_pairs={{126,0},{0,2},{2,4},{4,6},{6,8},{8,10},{10,12},{12,14},{14,16},{16... | collective-permute-start | bytes 6291464 | tf_op jit(solution)/shard_map/while/body/eval_jaxpr/ppermute | solution.py:19
  307.9 22.0 %reduce-scatter.5.cloned.1.call-start = ((), (), s32[]{:S(2)}) async-start(), calls=%async_computation.4 | async-start | bytes 196608 | tf_op jit(solution)/shard_map/while/body/eval_jaxpr/reduce_scatter | solution.py:77
  309.5 48.4 %collective-permute-start = (bf16[128,8192]{1,0:T(8,128)(2,1)S(1)}, bf16[128,8192]{1,0:T(8,128)(2,1)}, u32[]{:S(2)}, u32[]{:S(2)}) collective-permute-start(bf16[128,8192]{1,0:T(8,128)(2,1)S(1)} %copy.19), channel_id=1, source_target_pairs={{126,0},{0,2},{2,4},{4,6},{6,8},{8,10},{10,12},{12,14},{14,16},{16... | collective-permute-start | bytes 6291464 | tf_op jit(solution)/shard_map/while/body/eval_jaxpr/ppermute | solution.py:19
  357.9 22.9 %reduce-scatter.5.cloned.1.call-start = ((), (), s32[]{:S(2)}) async-start(), calls=%async_computation.4 | async-start | bytes 196608 | tf_op jit(solution)/shard_map/while/body/eval_jaxpr/reduce_scatter | solution.py:77
  359.5 47.5 %collective-permute-start = (bf16[128,8192]{1,0:T(8,128)(2,1)S(1)}, bf16[128,8192]{1,0:T(8,128)(2,1)}, u32[]{:S(2)}, u32[]{:S(2)}) collective-permute-start(bf16[128,8192]{1,0:T(8,128)(2,1)S(1)} %copy.19), channel_id=1, source_target_pairs={{126,0},{0,2},{2,4},{4,6},{6,8},{8,10},{10,12},{12,14},{14,16},{16... | collective-permute-start | bytes 6291464 | tf_op jit(solution)/shard_map/while/body/eval_jaxpr/ppermute | solution.py:19
  407.0 23.9 %reduce-scatter.5.cloned.1.call-start = ((), (), s32[]{:S(2)}) async-start(), calls=%async_computation.4 | async-start | bytes 196608 | tf_op jit(solution)/shard_map/while/body/eval_jaxpr/reduce_scatter | solution.py:77
  408.6 46.6 %collective-permute-start = (bf16[128,8192]{1,0:T(8,128)(2,1)S(1)}, bf16[128,8192]{1,0:T(8,128)(2,1)}, u32[]{:S(2)}, u32[]{:S(2)}) collective-permute-start(bf16[128,8192]{1,0:T(8,128)(2,1)S(1)} %copy.19), channel_id=1, source_target_pairs={{126,0},{0,2},{2,4},{4,6},{6,8},{8,10},{10,12},{12,14},{14,16},{16... | collective-permute-start | bytes 6291464 | tf_op jit(solution)/shard_map/while/body/eval_jaxpr/ppermute | solution.py:19
  455.1 24.8 %reduce-scatter.5.cloned.1.call-start = ((), (), s32[]{:S(2)}) async-start(), calls=%async_computation.4 | async-start | bytes 196608 | tf_op jit(solution)/shard_map/while/body/eval_jaxpr/reduce_scatter | solution.py:77
  456.7 45.6 %collective-permute-start = (bf16[128,8192]{1,0:T(8,128)(2,1)S(1)}, bf16[128,8192]{1,0:T(8,128)(2,1)}, u32[]{:S(2)}, u32[]{:S(2)}) collective-permute-start(bf16[128,8192]{1,0:T(8,128)(2,1)S(1)} %copy.19), channel_id=1, source_target_pairs={{126,0},{0,2},{2,4},{4,6},{6,8},{8,10},{10,12},{12,14},{14,16},{16... | collective-permute-start | bytes 6291464 | tf_op jit(solution)/shard_map/while/body/eval_jaxpr/ppermute | solution.py:19
  502.4 25.7 %reduce-scatter.5.cloned.1.call-start = ((), (), s32[]{:S(2)}) async-start(), calls=%async_computation.4 | async-start | bytes 196608 | tf_op jit(solution)/shard_map/while/body/eval_jaxpr/reduce_scatter | solution.py:77
  503.9 44.7 %collective-permute-start = (bf16[128,8192]{1,0:T(8,128)(2,1)S(1)}, bf16[128,8192]{1,0:T(8,128)(2,1)}, u32[]{:S(2)}, u32[]{:S(2)}) collective-permute-start(bf16[128,8192]{1,0:T(8,128)(2,1)S(1)} %copy.19), channel_id=1, source_target_pairs={{126,0},{0,2},{2,4},{4,6},{6,8},{8,10},{10,12},{12,14},{14,16},{16... | collective-permute-start | bytes 6291464 | tf_op jit(solution)/shard_map/while/body/eval_jaxpr/ppermute | solution.py:19
  548.7 26.6 %reduce-scatter.5.cloned.1.call-start = ((), (), s32[]{:S(2)}) async-start(), calls=%async_computation.4 | async-start | bytes 196608 | tf_op jit(solution)/shard_map/while/body/eval_jaxpr/reduce_scatter | solution.py:77
  550.3 43.8 %collective-permute-start = (bf16[128,8192]{1,0:T(8,128)(2,1)S(1)}, bf16[128,8192]{1,0:T(8,128)(2,1)}, u32[]{:S(2)}, u32[]{:S(2)}) collective-permute-start(bf16[128,8192]{1,0:T(8,128)(2,1)S(1)} %copy.19), channel_id=1, source_target_pairs={{126,0},{0,2},{2,4},{4,6},{6,8},{8,10},{10,12},{12,14},{14,16},{16... | collective-permute-start | bytes 6291464 | tf_op jit(solution)/shard_map/while/body/eval_jaxpr/ppermute | solution.py:19
  594.0 27.5 %reduce-scatter.5.cloned.1.call-start = ((), (), s32[]{:S(2)}) async-start(), calls=%async_computation.4 | async-start | bytes 196608 | tf_op jit(solution)/shard_map/while/body/eval_jaxpr/reduce_scatter | solution.py:77
  595.6 42.9 %collective-permute-start = (bf16[128,8192]{1,0:T(8,128)(2,1)S(1)}, bf16[128,8192]{1,0:T(8,128)(2,1)}, u32[]{:S(2)}, u32[]{:S(2)}) collective-permute-start(bf16[128,8192]{1,0:T(8,128)(2,1)S(1)} %copy.19), channel_id=1, source_target_pairs={{126,0},{0,2},{2,4},{4,6},{6,8},{8,10},{10,12},{12,14},{14,16},{16... | collective-permute-start | bytes 6291464 | tf_op jit(solution)/shard_map/while/body/eval_jaxpr/ppermute | solution.py:19
  638.5 28.9 %reduce-scatter.5.cloned.1.call-start = ((), (), s32[]{:S(2)}) async-start(), calls=%async_computation.4 | async-start | bytes 196608 | tf_op jit(solution)/shard_map/while/body/eval_jaxpr/reduce_scatter | solution.py:77
  640.1 42.5 %collective-permute-start = (bf16[128,8192]{1,0:T(8,128)(2,1)S(1)}, bf16[128,8192]{1,0:T(8,128)(2,1)}, u32[]{:S(2)}, u32[]{:S(2)}) collective-permute-start(bf16[128,8192]{1,0:T(8,128)(2,1)S(1)} %copy.19), channel_id=1, source_target_pairs={{126,0},{0,2},{2,4},{4,6},{6,8},{8,10},{10,12},{12,14},{14,16},{16... | collective-permute-start | bytes 6291464 | tf_op jit(solution)/shard_map/while/body/eval_jaxpr/ppermute | solution.py:19
  682.6 30.6 %reduce-scatter.5.cloned.1.call-start = ((), (), s32[]{:S(2)}) async-start(), calls=%async_computation.4 | async-start | bytes 196608 | tf_op jit(solution)/shard_map/while/body/eval_jaxpr/reduce_scatter | solution.py:77
  684.2 42.5 %collective-permute-start = (bf16[128,8192]{1,0:T(8,128)(2,1)S(1)}, bf16[128,8192]{1,0:T(8,128)(2,1)}, u32[]{:S(2)}, u32[]{:S(2)}) collective-permute-start(bf16[128,8192]{1,0:T(8,128)(2,1)S(1)} %copy.19), channel_id=1, source_target_pairs={{126,0},{0,2},{2,4},{4,6},{6,8},{8,10},{10,12},{12,14},{14,16},{16... | collective-permute-start | bytes 6291464 | tf_op jit(solution)/shard_map/while/body/eval_jaxpr/ppermute | solution.py:19
  726.7 32.3 %reduce-scatter.5.cloned.1.call-start = ((), (), s32[]{:S(2)}) async-start(), calls=%async_computation.4 | async-start | bytes 196608 | tf_op jit(solution)/shard_map/while/body/eval_jaxpr/reduce_scatter | solution.py:77
  728.3 42.5 %collective-permute-start = (bf16[128,8192]{1,0:T(8,128)(2,1)S(1)}, bf16[128,8192]{1,0:T(8,128)(2,1)}, u32[]{:S(2)}, u32[]{:S(2)}) collective-permute-start(bf16[128,8192]{1,0:T(8,128)(2,1)S(1)} %copy.19), channel_id=1, source_target_pairs={{126,0},{0,2},{2,4},{4,6},{6,8},{8,10},{10,12},{12,14},{14,16},{16... | collective-permute-start | bytes 6291464 | tf_op jit(solution)/shard_map/while/body/eval_jaxpr/ppermute | solution.py:19
  770.8 34.0 %reduce-scatter.5.cloned.1.call-start = ((), (), s32[]{:S(2)}) async-start(), calls=%async_computation.4 | async-start | bytes 196608 | tf_op jit(solution)/shard_map/while/body/eval_jaxpr/reduce_scatter | solution.py:77
  772.4 42.5 %collective-permute-start = (bf16[128,8192]{1,0:T(8,128)(2,1)S(1)}, bf16[128,8192]{1,0:T(8,128)(2,1)}, u32[]{:S(2)}, u32[]{:S(2)}) collective-permute-start(bf16[128,8192]{1,0:T(8,128)(2,1)S(1)} %copy.19), channel_id=1, source_target_pairs={{126,0},{0,2},{2,4},{4,6},{6,8},{8,10},{10,12},{12,14},{14,16},{16... | collective-permute-start | bytes 6291464 | tf_op jit(solution)/shard_map/while/body/eval_jaxpr/ppermute | solution.py:19
  814.8 23.4 %reduce-scatter.3.cloned.1.call-start = ((), (), s32[]{:S(2)}) async-start(), calls=%async_computation.3 | async-start | bytes 196608 | tf_op jit(solution)/shard_map/reduce_scatter | solution.py:77
  (4 other events, 41.2 us)
Sparse Core Ops, SparseCore 0:
  106.5 12.0 reduce-scatter.4
  159.5 12.1 reduce-scatter.4
  212.2 13.0 reduce-scatter.4
  264.1 13.9 reduce-scatter.4
  315.0 14.9 reduce-scatter.4
  365.0 15.8 reduce-scatter.4
  414.0 16.7 reduce-scatter.4
  462.2 17.6 reduce-scatter.4
  509.4 18.6 reduce-scatter.4
  555.7 19.5 reduce-scatter.4
  601.1 20.4 reduce-scatter.4
  645.5 21.8 reduce-scatter.4
  689.6 23.5 reduce-scatter.4
  733.7 25.2 reduce-scatter.4
  777.8 26.9 reduce-scatter.4
Sparse Core Ops, SparseCore 1:
  820.9 17.3 reduce-scatter.2
where the time goes:
time: 852 us; the launch traced here: 849 us
  waiting for transfers between devices  604 us (71%)
  matrix products  86.1 us (10%)
  other arithmetic  79 us (9%)
  local copies, waits for them, and re-layouts  49 us (6%)
  between operations  14.7 us (2%)
  starting transfers between devices  12.5 us (1%)
    ppermute x15, waiting for transfers between devices, from_behind(): return lax.ppermute(block, axis, route)  314 us
    reduce_scatter x16, waiting for transfers between devices, correlate(): lax.psum_scatter(jnp.dot(receivers, kernel, preferred_element_type=jnp.fl...  290 us
    dot_general x16, matrix products, correlate(): jnp.dot(receivers, kernel, preferred_element_type=jnp.float32)  85.4 us
    another operation x15, local copies, waits for them, and re-layouts  23.9 us
    add x1, other arithmetic, per_device(): kernel_real = real_part * cosine_table + imag_part * sine_table  22.5 us
    dynamic_update_slice x15, other arithmetic, per_device(): lax.scan(advance, resident, None, length=cycle_steps - 1)  22.4 us
  transfers between devices with their start and end apart: 32, of which 31 were waited for; matrix products, arithmetic and copies ran while one was open for 19% of the time, Pallas kernels for 0%

commit v1 on v0

v1 whole, which is shorter than its diff:
```python
import functools
import math

import jax
import jax.numpy as jnp
import numpy as np
from jax import lax
from jax.experimental import pallas as pl
from jax.experimental.pallas import tpu as pltpu
from jax.sharding import PartitionSpec as P

BINS = 8192
DEC = 8
OUT = 256
EPS = 1e-06
Q = 16
PERIOD = BINS // DEC
LANES = 128
SIDE = 4
ROWS = BINS // LANES
GROUP = 8
PARTS = ((0, 48), (48, 96), (96, 128))
ORDERS = ((2, 1, 0), (1, 0, 2), (0, 2, 1))


def lag_table():
    bins = np.arange(PERIOD)[:, None]
    lags = np.arange(OUT)[None, :] - OUT // 2
    angle = 2.0 * np.pi * ((bins * lags) % PERIOD) / PERIOD
    shape = (PERIOD // LANES, LANES, OUT)
    both = [np.cos(angle).reshape(shape), np.sin(angle).reshape(shape)]
    return (np.concatenate(both, axis=1) / math.sqrt(BINS)).astype(jnp.bfloat16)


def whiten(block):
    values = block.astype(jnp.float32)
    total = jnp.sum(jnp.sum(values * values, axis=0, keepdims=True), axis=1, keepdims=True)
    return (values * lax.rsqrt(total / (2 * BINS) + EPS)).astype(jnp.bfloat16)


def fused(
    idx,
    x_in,
    s_in,
    table,
    recv,
    xs,
    raw,
    sb,
    ca,
    cb,
    stage,
    pair_send,
    pair_recv,
    local_sem,
    ring_send,
    ring_recv,
    out_send,
    out_recv,
    twin_send,
):
    blk = lax.axis_index("blk")
    band = lax.axis_index("band")
    blocks = SIDE**3
    stations = x_in.shape[0]
    half = ROWS // 2
    place = [blk // 16, (blk // 4) % 4, blk % 4]

    def device(coords, core):
        return ((coords[0] * SIDE + coords[1]) * SIDE + coords[2], core)

    def remote(src, dst, send, recv_sem, target):
        return pltpu.make_async_remote_copy(
            src_ref=src,
            dst_ref=dst,
            send_sem=send,
            recv_sem=recv_sem,
            device_id=target,
            device_id_type=pl.DeviceIdType.MESH,
        )

    mine = pl.ds(pl.multiple_of(band * half, half), half)
    other = pl.ds(pl.multiple_of((1 - band) * half, half), half)
    twin = (blk, 1 - band)

    source_out = remote(
        s_in.at[1 - band], raw.at[:, mine, :], pair_send.at[0], pair_recv.at[0], twin
    )
    source_out.start()
    source_keep = pltpu.make_async_copy(s_in.at[band], raw.at[:, mine, :], local_sem.at[0])
    source_keep.start()
    station_out = remote(
        x_in, xs.at[pl.ds(0, stations), :, mine, :], pair_send.at[1], pair_recv.at[1], twin
    )
    station_out.start()
    station_keep = pltpu.make_async_copy(
        x_in, xs.at[pl.ds(0, stations), :, mine, :], local_sem.at[1]
    )
    station_keep.start()
    xs[stations] = jnp.zeros(xs.shape[1:], xs.dtype)

    source_keep.wait()
    source_out.wait_recv()
    source = raw[...].reshape(2 * ROWS, LANES)
    sb[place[0], place[1], place[2]] = whiten(source)

    pending = [source_out, station_out]

    def region(coords, rows):
        return sb.at[tuple(coords) + (pl.ds(rows[0], rows[1] - rows[0]), slice(None))]

    def moved(axis, step):
        coords = list(place)
        coords[axis] = (coords[axis] + step) % SIDE
        return coords

    def held(part, level):
        coords = list(place)
        for axis in ORDERS[part][:level]:
            coords[axis] = slice(None)
        return coords

    def ring_copy(part, level, way, coords, step):
        axis = ORDERS[part][level]
        spot = (part * 3 + level) * 4 + way
        return remote(
            region(coords, PARTS[part]),
            region(coords, PARTS[part]),
            ring_send.at[spot],
            ring_recv.at[spot],
            device(moved(axis, step), band),
        )

    def with_axis(coords, axis, value):
        coords = list(coords)
        coords[axis] = value
        return coords

    def start_level(part, level):
        coords = held(part, level)
        steps = (1, -1, 2) if level < 2 else (1, -1)
        for way, step in enumerate(steps):
            copy = ring_copy(part, level, way, coords, step)
            copy.start()
            pending.append(copy)

    def wait_way(part, level, way, step, half_axis=None, half_at=None):
        axis = ORDERS[part][level]
        coords = with_axis(held(part, level), axis, (place[axis] + step) % SIDE)
        if half_axis is not None:
            coords[half_axis] = pl.ds(half_at, SIDE // 2)
        ring_copy(part, level, way, coords, 1).wait_recv()

    for part in range(3):
        start_level(part, 0)
    for level in (0, 1):
        for part in range(3):
            for way, step in enumerate((-1, 1, 2)):
                wait_way(part, level, way, step)
            start_level(part, level + 1)

    station_keep.wait()
    station_out.wait_recv()

    @pl.loop(0, stations)
    def _(i):
        xs[i] = whiten(xs[i].reshape(2 * ROWS, LANES)).reshape(2, ROWS, LANES)

    for part in range(3):
        axis = ORDERS[part][2]
        split = ORDERS[part][0]
        for way, (come, go, at) in enumerate(((-1, 1, 0), (1, -1, 2))):
            wait_way(part, 2, way, come)
            coords = with_axis(held(part, 2), axis, (place[axis] + come) % SIDE)
            coords[split] = pl.ds(at, SIDE // 2)
            copy = ring_copy(part, 2, 2 + way, coords, go)
            copy.start()
            pending.append(copy)
    for part in range(3):
        split = ORDERS[part][0]
        wait_way(part, 2, 2, 2, split, 0)
        wait_way(part, 2, 3, 2, split, 2)

    side = blk // (blocks // 2)
    row = blk % (blocks // 2)

    def target(turn):
        coords = [
            (place[0] + turn // 16) % SIDE,
            (place[1] + (turn // 4) % 4) % SIDE,
            (place[2] + turn % 4) % SIDE,
        ]
        return coords, (coords[0] * SIDE + coords[1]) * SIDE + coords[2]

    @pl.loop(0, blocks // GROUP)
    def _(group):
        @pl.loop(0, GROUP)
        def _(member):
            coords, a = target(group * GROUP + member)
            real = sb[coords[0], coords[1], coords[2], pl.ds(0, ROWS), :]
            imag = sb[coords[0], coords[1], coords[2], pl.ds(ROWS, ROWS), :]

            @pl.loop(0, 2 * Q, unroll=4)
            def _(slot):
                b = (a + blocks - slot % Q) % blocks
                i = idx[(slot // Q) * blocks + b]
                xr = xs[i, 0]
                xi = xs[i, 1]
                at = pl.ds(pl.multiple_of((member * 2 * Q + slot) * 8, 8), 8)
                for out, prod in ((ca, xr * real + xi * imag), (cb, xr * imag - xi * real)):
                    fold = (prod[0:16] + prod[16:32]) + (prod[32:48] + prod[48:64])
                    fold = fold.astype(jnp.float32)
                    out[at, :] = fold[0:8] + fold[8:16]

        lags = jnp.zeros((GROUP * 2 * Q, OUT), jnp.float32)
        for k in range(PERIOD // LANES):
            pick = pl.ds(k, GROUP * 2 * Q, stride=8)
            left = jnp.concatenate([ca[pick, :], cb[pick, :]], axis=1).astype(jnp.bfloat16)
            lags += jnp.dot(left, table[k], preferred_element_type=jnp.float32)
        stage[pl.ds(group * GROUP, GROUP)] = lags.astype(jnp.bfloat16).reshape(GROUP, 2 * Q, OUT)

        @pl.loop(0, GROUP)
        def _(member):
            turn = group * GROUP + member
            _, a = target(turn)

            @pl.when(turn > 0)
            def _():
                remote(
                    stage.at[turn], recv.at[row, band], out_send, out_recv, (a, side)
                ).start()

    @pl.when(side == band)
    def _():
        pltpu.make_async_copy(stage.at[0], recv.at[row, band], out_recv).start()

    @pl.when(side != band)
    def _():
        copy = remote(stage.at[0], recv.at[row, band], twin_send, out_recv, twin)
        copy.start()
        copy.wait_send()

    for copy in pending:
        copy.wait_send()
    pltpu.make_async_copy(
        stage.at[pl.ds(1, blocks - 1)], stage.at[pl.ds(1, blocks - 1)], out_send
    ).wait()
    pltpu.make_async_copy(recv, recv, out_recv).wait()


def unscramble(recv, out):
    for c in range(recv.shape[0]):
        value = recv[c, 0].astype(jnp.float32)
        for arrival in range(2):
            out[pl.ds(2 * c + arrival, Q, stride=64), :] = value[arrival * Q : (arrival + 1) * Q]


def per_device(traces, sources, owner):
    stations = traces.shape[0]
    blocks = lax.axis_size("blk")
    x_in = traces.reshape(stations, 2, ROWS // 2, LANES)
    s_in = sources.reshape(2, 2, ROWS // 2, LANES)
    owners = owner[:, 0]
    hits = owners[None, :] == jnp.arange(blocks, dtype=jnp.int32)[:, None]
    numbers = jnp.arange(stations, dtype=jnp.int32)[None, :]
    first = jnp.min(jnp.where(hits, numbers, stations), axis=1)
    last = jnp.max(jnp.where(hits, numbers, -1), axis=1)
    idx = jnp.concatenate([first, jnp.where(last > first, last, stations)])
    table = jnp.asarray(lag_table())
    vmem = pl.BlockSpec(memory_space=pltpu.VMEM)
    recv = pl.pallas_call(
        fused,
        out_shape=jax.ShapeDtypeStruct((blocks // 2, 2, 2 * Q, OUT), jnp.bfloat16),
        in_specs=[
            pl.BlockSpec(memory_space=pltpu.SMEM),
            pl.BlockSpec(memory_space=pl.ANY),
            pl.BlockSpec(memory_space=pl.ANY),
            vmem,
        ],
        out_specs=vmem,
        scratch_shapes=[
            pltpu.VMEM((stations + 1, 2, ROWS, LANES), jnp.bfloat16),
            pltpu.VMEM((2, ROWS, LANES), jnp.bfloat16),
            pltpu.VMEM((SIDE, SIDE, SIDE, 2 * ROWS, LANES), jnp.bfloat16),
            pltpu.VMEM((GROUP * 2 * Q * 8, LANES), jnp.float32),
            pltpu.VMEM((GROUP * 2 * Q * 8, LANES), jnp.float32),
            pltpu.VMEM((blocks, 2 * Q, OUT), jnp.bfloat16),
            pltpu.SemaphoreType.DMA((2,)),
            pltpu.SemaphoreType.DMA((2,)),
            pltpu.SemaphoreType.DMA((2,)),
            pltpu.SemaphoreType.DMA((36,)),
            pltpu.SemaphoreType.DMA((36,)),
            pltpu.SemaphoreType.DMA,
            pltpu.SemaphoreType.DMA,
            pltpu.SemaphoreType.DMA,
        ],
        compiler_params=pltpu.CompilerParams(
            has_side_effects=True, vmem_limit_bytes=40 * 1024 * 1024
        ),
        name="correlate",
    )(idx, x_in, s_in, table)
    out = pl.pallas_call(
        unscramble,
        grid=(2, 2),
        out_shape=jax.ShapeDtypeStruct((2 * Q * 64, OUT), jnp.float32),
        in_specs=[pl.BlockSpec((blocks // 2, 1, 2 * Q, LANES), lambda s, l: (0, s, 0, l))],
        out_specs=pl.BlockSpec((Q * 64, LANES), lambda s, l: (s, l)),
        name="unscramble",
    )(recv)
    return out.reshape(2, Q, 64, OUT)


def solution(mesh):
    placed = (P("blk", None, "band"), P("blk", None, "band"), P("blk", None))
    return jax.shard_map(
        per_device,
        mesh=mesh,
        in_specs=placed,
        out_specs=P("blk", None, "band", None),
        check_vma=False,
    )
```

time: 852 us -> 88.2 us (0.10)
  the two profiles are of different devices: /device:TPU:1 before, /device:TPU:0 now
where the time goes in v1:
time: 88.2 us; the launch traced here: 87.9 us
  Pallas kernels  83.3 us (94%)
  local copies, waits for them, and re-layouts  3.63 us (4%)
  other arithmetic  0.94 us (1%)
    pallas_call x1, Pallas kernels, per_device(): pl.pallas_call(fused, out_shape=jax.ShapeDtypeStruct((blocks // 2, 2, 2 *...  79 us
    pallas_call x1, Pallas kernels, per_device(): pl.pallas_call(unscramble, grid=(2, 2), out_shape=jax.ShapeDtypeStruct((2...  4.35 us
    reshape x1, local copies, waits for them, and re-layouts, per_device(): x_in = traces.reshape(stations, 2, ROWS // 2, LANES)  1.85 us

profile of v1, /device:TPU:0, one launch (start us, length us, event | category | flops | bytes accessed | tf_op | source)
XLA Modules:
  0.0 87.9 jit_solution(3863858189937729890)
XLA Ops:
  0.0 0.0 copy-start.1
  0.0 0.9 select_reduce_fusion.1
  0.9 0.1 pad_add_fusion.idx
  1.0 0.8 reshape.11.s_in
  1.8 1.9 %reshape.10.x_in = bf16[64,2,32,128]{3,2,1,0:T(8,128)(2,1)S(1)} reshape(bf16[64,2,4096]{2,1,0:T(2,128)(2,1)} %param.4) | data formatting | bytes 2097152 | tf_op jit(solution)/shard_map/reshape | solution.py:261
  3.6 0.0 copy-done.1
  3.6 79.0 %correlate.1.recv = bf16[32,2,32,256]{3,2,1,0:T(8,128)(2,1)S(1)} custom-call(s32[128]{0:T(128)S(1)} %pad_add_fusion.idx, bf16[64,2,32,128]{3,2,1,0:T(8,128)(2,1)S(1)} %reshape.10.x_in, bf16[2,2,32,128]{3,2,1,0:T(8,128)(2,1)S(1)} %reshape.11.s_in, bf16[8,256,256]{2,1,0:T(8,128)(2,1)S(1)} %copy-done.1), custom_call_target="tpu_custom_call" | custom-call | tf_op jit(solution)/shard_map/correlate/pallas_call | solution.py:271
  82.6 0.0 copy-start
  82.6 1.0 %copy-done = bf16[32,2,32,256]{3,2,1,0:T(8,128)(2,1)} copy-done((bf16[32,2,32,256]{3,2,1,0:T(8,128)(2,1)}, bf16[32,2,32,256]{3,2,1,0:T(8,128)(2,1)S(1)}, u32[]{:S(2)}) %copy-start) | copy-done | bytes 1048600
  83.6 4.3 %unscramble.1 = f32[2048,256]{1,0:T(8,128)} custom-call(bf16[32,2,32,256]{3,2,1,0:T(8,128)(2,1)} %copy-done), custom_call_target="tpu_custom_call" | custom-call | tf_op jit(solution)/shard_map/unscramble/pallas_call | solution.py:302
  (1 shorter events, 0.0 us)
Async XLA Ops:
  0.0 3.6 %copy-start.1 = (bf16[8,256,256]{2,1,0:T(8,128)(2,1)S(1)}, bf16[8,256,256]{2,1,0:T(8,128)(2,1)}, u32[]{:S(2)}) copy-start(bf16[8,256,256]{2,1,0:T(8,128)(2,1)} %constant.10.clone.table) | copy-start | bytes 3145732
  82.6 1.0 %copy-start = (bf16[32,2,32,256]{3,2,1,0:T(8,128)(2,1)}, bf16[32,2,32,256]{3,2,1,0:T(8,128)(2,1)S(1)}, u32[]{:S(2)}) copy-start(bf16[32,2,32,256]{3,2,1,0:T(8,128)(2,1)S(1)} %correlate.1.recv) | copy-start | bytes 3145732

commit v2 on v1

v2 whole, which is shorter than its diff:
```python
import math

import jax
import jax.numpy as jnp
import numpy as np
from jax import lax
from jax.experimental import pallas as pl
from jax.experimental.pallas import tpu as pltpu
from jax.sharding import PartitionSpec as P

BINS = 8192
DEC = 8
OUT = 256
EPS = 1e-06
Q = 16
PERIOD = BINS // DEC
LANES = 128
SIDE = 4
ROWS = BINS // LANES
GROUP = 8
PATH = (
    ((0, 0), None),
    ((1, 0), (1, 0)),
    ((3, 0), (3, 0)),
    ((0, 1), (0, 1)),
    ((0, 3), (0, 3)),
    ((1, 1), (1, 0)),
    ((3, 3), (3, 0)),
    ((3, 1), (0, 1)),
    ((1, 3), (0, 3)),
    ((2, 0), (1, 0)),
    ((2, 1), (3, 0)),
    ((0, 2), (0, 1)),
    ((1, 2), (0, 3)),
    ((2, 2), (1, 0)),
    ((3, 2), (3, 0)),
    ((2, 3), (0, 3)),
)
ROUNDS = {1: range(1, 5), 4: range(5, 9), 7: range(9, 13), 10: range(13, 16)}


def lag_table():
    bins = np.arange(PERIOD)[:, None]
    lags = np.arange(OUT)[None, :] - OUT // 2
    angle = 2.0 * np.pi * ((bins * lags) % PERIOD) / PERIOD
    shape = (PERIOD // LANES, LANES, OUT)
    both = [np.cos(angle).reshape(shape), np.sin(angle).reshape(shape)]
    return (np.concatenate(both, axis=1) / math.sqrt(BINS)).astype(jnp.bfloat16)


def whiten(values):
    total = jnp.sum(jnp.sum(values * values, axis=(0, 1), keepdims=True), axis=2, keepdims=True)
    return (values * lax.rsqrt(total / (2 * BINS) + EPS)).astype(jnp.bfloat16)


def fold(products):
    pairs = (products[0:16] + products[16:32]) + (products[32:48] + products[48:64])
    pairs = pairs.astype(jnp.float32)
    return pairs[0:8] + pairs[8:16]


def correlate(
    idx,
    x_in,
    s_in,
    table,
    recv,
    raw,
    xs,
    source,
    sb,
    ca,
    cb,
    stage,
    pair_send,
    pair_recv,
    local_sem,
    ring_send,
    ring_recv,
    out_send,
    out_recv,
    twin_send,
):
    blk = lax.axis_index("blk")
    band = lax.axis_index("band")
    blocks = SIDE**3
    stations = x_in.shape[0]
    half = ROWS // 2
    pz, py, px = blk // 16, (blk // 4) % 4, blk % 4
    twin = (blk, 1 - band)

    def device(dy, dz, dx):
        z, y, x = (pz + dz) & 3, (py + dy) & 3, (px + dx) & 3
        return ((z * SIDE + y) * SIDE + x, band)

    def remote(src, dst, send, recv_sem, target):
        return pltpu.make_async_remote_copy(
            src_ref=src,
            dst_ref=dst,
            send_sem=send,
            recv_sem=recv_sem,
            device_id=target,
            device_id_type=pl.DeviceIdType.MESH,
        )

    barrier = pltpu.get_barrier_semaphore()
    greeted = [twin]
    for step in (1, 2, 3):
        greeted += [device(step, 0, 0), device(0, step, 0), device(0, 0, step)]
    greeted = [g for n, g in enumerate(greeted) if n not in (4, 5)]
    for target in greeted:
        pl.semaphore_signal(barrier, inc=1, device_id=target, device_id_type=pl.DeviceIdType.MESH)

    mine = pl.ds(pl.multiple_of(band * half, half), half)
    source_keep = pltpu.make_async_copy(s_in.at[band], source.at[:, mine, :], local_sem.at[0])
    source_keep.start()
    station_keep = pltpu.make_async_copy(x_in, raw.at[:, :, mine, :], local_sem.at[1])
    station_keep.start()
    xs[stations] = jnp.zeros(xs.shape[1:], xs.dtype)
    pl.semaphore_wait(barrier, len(greeted))

    source_out = remote(
        s_in.at[1 - band], source.at[:, mine, :], pair_send.at[0], pair_recv.at[0], twin
    )
    source_out.start()
    station_out = remote(x_in, raw.at[:, :, mine, :], pair_send.at[1], pair_recv.at[1], twin)
    station_out.start()
    source_keep.wait()
    source_out.wait_recv()
    own = whiten(source[...].astype(jnp.float32))
    sb[pz, py, px] = own.reshape(2 * ROWS, LANES)
    pending = [source_out, station_out]

    def x_copy(step, at):
        block = sb.at[pz, py, at]
        return remote(
            block, block, ring_send.at[15 + step - 1], ring_recv.at[15 + step - 1], device(0, 0, step)
        )

    for step in (1, 3, 2):
        copy = x_copy(step, px)
        copy.start()
        pending.append(copy)
    for step in (1, 3, 2):
        x_copy(step, (px + 4 - step) & 3).wait_recv()

    def row_copy(n, place):
        row = sb.at[(pz + 4 - place[1]) & 3, (py + 4 - place[0]) & 3]
        step = PATH[n][1]
        return remote(
            row, row, ring_send.at[n - 1], ring_recv.at[n - 1], device(step[0], step[1], 0)
        )

    def pass_on(n):
        place = PATH[n][0]
        for child in range(1, 16):
            there, step = PATH[child]
            if ((there[0] - step[0]) % 4, (there[1] - step[1]) % 4) == place:
                row_copy(child, place).start()

    pass_on(0)

    station_keep.wait()
    station_out.wait_recv()

    @pl.loop(0, stations // 8)
    def _(group):
        for member in range(8):
            i = group * 8 + member
            white = whiten(raw[i].astype(jnp.float32))
            xs[i, 0:2] = white
            xs[i, 2] = white[0] + white[1]

    side = blk // (blocks // 2)
    row = blk % (blocks // 2)

    def block_at(turn):
        n, x = turn // SIDE, turn % SIDE
        dy, dz = 0, 0
        for k in range(1, 16):
            (ky, kz), _ = PATH[k]
            dy += jnp.where(n == k, ky, 0)
            dz += jnp.where(n == k, kz, 0)
        return (pz + 4 - dz) & 3, (py + 4 - dy) & 3, (px + x) & 3

    @pl.loop(0, blocks // SIDE)
    def _(n):
        for when, arrivals in ROUNDS.items():

            @pl.when(n == when)
            def _():
                for k in arrivals:
                    row_copy(k, PATH[k][0]).wait_recv()
                    pass_on(k)

        @pl.loop(0, SIDE)
        def _(x):
            az, ay, ax = block_at(n * SIDE + x)
            a = (az * SIDE + ay) * SIDE + ax
            real = sb[az, ay, ax, pl.ds(0, ROWS), :]
            imag = sb[az, ay, ax, pl.ds(ROWS, ROWS), :]
            less = real - imag
            more = real + imag
            base = ((n % 2) * SIDE + x) * (2 * Q * 8)
            for slot in range(2 * Q):
                i = idx[(slot // Q) * blocks + ((a + blocks - slot % Q) & (blocks - 1))]
                k1 = fold(xs[i, 2] * imag)
                k2 = fold(xs[i, 0] * less)
                k3 = fold(xs[i, 1] * more)
                at = pl.ds(pl.multiple_of(base + slot * 8, 8), 8)
                ca[at, :] = k1 + k2
                cb[at, :] = k1 - k3

        @pl.when(n % 2 == 1)
        def _():
            lags = jnp.zeros((GROUP * 2 * Q, OUT), jnp.float32)
            for k in range(PERIOD // LANES):
                pick = pl.ds(k, GROUP * 2 * Q, stride=8)
                left = jnp.concatenate([ca[pick, :], cb[pick, :]], axis=1).astype(jnp.bfloat16)
                lags += jnp.dot(left, table[k], preferred_element_type=jnp.float32)
            first = (n // 2) * GROUP
            stage[pl.ds(first, GROUP)] = lags.astype(jnp.bfloat16).reshape(GROUP, 2 * Q, OUT)

            @pl.loop(0, GROUP)
            def _(member):
                turn = first + member
                az, ay, ax = block_at(turn)

                @pl.when(turn > 0)
                def _():
                    remote(
                        stage.at[turn],
                        recv.at[row, band],
                        out_send,
                        out_recv,
                        ((az * SIDE + ay) * SIDE + ax, side),
                    ).start()

    @pl.when(side == band)
    def _():
        pltpu.make_async_copy(stage.at[0], recv.at[row, band], out_recv).start()

    @pl.when(side != band)
    def _():
        copy = remote(stage.at[0], recv.at[row, band], twin_send, out_recv, twin)
        copy.start()
        copy.wait_send()

    for copy in pending:
        copy.wait_send()
    for n in range(1, 16):
        row_copy(n, PATH[n][0]).wait_send()
    pltpu.make_async_copy(
        stage.at[pl.ds(1, blocks - 1)], stage.at[pl.ds(1, blocks - 1)], out_send
    ).wait()
    pltpu.make_async_copy(recv, recv, out_recv).wait()


def unscramble(recv, out, wide, sem):
    to = lax.broadcasted_iota(jnp.int32, (256, 256), 0)
    at = lax.broadcasted_iota(jnp.int32, (256, 256), 1)
    move = ((to % 16) * 16 + to // 16 == at).astype(jnp.bfloat16)
    copies = []
    for s in range(2):
        for g in range(4):
            value = recv[8 * g : 8 * g + 8, s].reshape(256, OUT)
            value = jnp.dot(move, value, preferred_element_type=jnp.float32)
            wide[s, :, 16 * g : 16 * g + 16, :] = value.reshape(Q, 16, OUT)
        copy = pltpu.make_async_copy(wide.at[s], out.at[s], sem.at[s])
        copy.start()
        copies.append(copy)
    for copy in copies:
        copy.wait()


def per_device(traces, sources, owner):
    stations = traces.shape[0]
    blocks = lax.axis_size("blk")
    x_in = traces.reshape(stations, 2, ROWS // 2, LANES)
    s_in = sources.reshape(2, 2, ROWS // 2, LANES)
    owners = owner[:, 0]
    hits = owners[None, :] == jnp.arange(blocks, dtype=jnp.int32)[:, None]
    numbers = jnp.arange(stations, dtype=jnp.int32)[None, :]
    first = jnp.min(jnp.where(hits, numbers, stations), axis=1)
    last = jnp.max(jnp.where(hits, numbers, -1), axis=1)
    idx = jnp.concatenate([first, jnp.where(last > first, last, stations)])
    table = jnp.asarray(lag_table())
    vmem = pl.BlockSpec(memory_space=pltpu.VMEM)
    recv = pl.pallas_call(
        correlate,
        out_shape=jax.ShapeDtypeStruct((blocks // 2, 2, 2 * Q, OUT), jnp.bfloat16),
        in_specs=[
            pl.BlockSpec(memory_space=pltpu.SMEM),
            pl.BlockSpec(memory_space=pl.ANY),
            pl.BlockSpec(memory_space=pl.ANY),
            vmem,
        ],
        out_specs=vmem,
        scratch_shapes=[
            pltpu.VMEM((stations, 2, ROWS, LANES), jnp.bfloat16),
            pltpu.VMEM((stations + 1, 3, ROWS, LANES), jnp.bfloat16),
            pltpu.VMEM((2, ROWS, LANES), jnp.bfloat16),
            pltpu.VMEM((SIDE, SIDE, SIDE, 2 * ROWS, LANES), jnp.bfloat16),
            pltpu.VMEM((GROUP * 2 * Q * 8, LANES), jnp.float32),
            pltpu.VMEM((GROUP * 2 * Q * 8, LANES), jnp.float32),
            pltpu.VMEM((blocks, 2 * Q, OUT), jnp.bfloat16),
            pltpu.SemaphoreType.DMA((2,)),
            pltpu.SemaphoreType.DMA((2,)),
            pltpu.SemaphoreType.DMA((2,)),
            pltpu.SemaphoreType.DMA((18,)),
            pltpu.SemaphoreType.DMA((18,)),
            pltpu.SemaphoreType.DMA,
            pltpu.SemaphoreType.DMA,
            pltpu.SemaphoreType.DMA,
        ],
        compiler_params=pltpu.CompilerParams(
            has_side_effects=True, collective_id=0, vmem_limit_bytes=40 * 1024 * 1024
        ),
        name="correlate",
    )(idx, x_in, s_in, table)
    return pl.pallas_call(
        unscramble,
        out_shape=jax.ShapeDtypeStruct((2, Q, 64, OUT), jnp.float32),
        in_specs=[vmem],
        out_specs=pl.BlockSpec(memory_space=pl.ANY),
        scratch_shapes=[
            pltpu.VMEM((2, Q, 64, OUT), jnp.float32),
            pltpu.SemaphoreType.DMA((2,)),
        ],
        name="unscramble",
    )(recv)


def solution(mesh):
    placed = (P("blk", None, "band"), P("blk", None, "band"), P("blk", None))
    return jax.shard_map(
        per_device,
        mesh=mesh,
        in_specs=placed,
        out_specs=P("blk", None, "band", None),
        check_vma=False,
    )
```

time: 88.2 us -> 61.3 us (0.70)
  the two profiles are of different devices: /device:TPU:0 before, /device:TPU:1 now
where the time goes in v2:
time: 61.3 us; the launch traced here: 61.1 us
  Pallas kernels  56.5 us (92%)
  local copies, waits for them, and re-layouts  3.63 us (6%)
  other arithmetic  0.94 us (2%)
    pallas_call x1, Pallas kernels, per_device(): pl.pallas_call(correlate, out_shape=jax.ShapeDtypeStruct((blocks // 2, 2,...  53.6 us
    pallas_call x1, Pallas kernels, per_device(): pl.pallas_call(unscramble, out_shape=jax.ShapeDtypeStruct((2, Q, 64, OUT)...  2.86 us
    reshape x1, local copies, waits for them, and re-layouts, per_device(): x_in = traces.reshape(stations, 2, ROWS // 2, LANES)  1.85 us

profile of v2, /device:TPU:1, one launch (start us, length us, event | category | flops | bytes accessed | tf_op | source)
XLA Modules:
  0.0 61.1 jit_solution(15660404291888588982)
XLA Ops:
  0.0 0.0 copy-start.1
  0.0 0.9 %select_reduce_fusion.1 = (s32[64]{0:T(128)S(1)}, s32[64]{0:T(128)S(1)}) fusion(s32[64]{0:T(128)} %bitcast.1), kind=kLoop, calls=%fused_computation.1 | loop fusion | flops 20352 | bytes 768 | tf_op jit(solution)/shard_map/reduce_min | solution.py:284
  0.9 0.1 pad_add_fusion.idx
  1.0 0.8 %reshape.8.s_in = bf16[2,2,32,128]{3,2,1,0:T(8,128)(2,1)S(1)} reshape(bf16[2,2,4096]{2,1,0:T(2,128)(2,1)} %param.5) | data formatting | bytes 65536 | tf_op jit(solution)/shard_map/reshape | solution.py:280
  1.8 1.9 %reshape.7.x_in = bf16[64,2,32,128]{3,2,1,0:T(8,128)(2,1)S(1)} reshape(bf16[64,2,4096]{2,1,0:T(2,128)(2,1)} %param.4) | data formatting | bytes 2097152 | tf_op jit(solution)/shard_map/reshape | solution.py:279
  3.6 0.0 copy-done.1
  3.6 53.6 %correlate.1.recv = bf16[32,2,32,256]{3,2,1,0:T(8,128)(2,1)S(1)} custom-call(s32[128]{0:T(128)S(1)} %pad_add_fusion.idx, bf16[64,2,32,128]{3,2,1,0:T(8,128)(2,1)S(1)} %reshape.7.x_in, bf16[2,2,32,128]{3,2,1,0:T(8,128)(2,1)S(1)} %reshape.8.s_in, bf16[8,256,256]{2,1,0:T(8,128)(2,1)S(1)} %copy-done.1), custom_call_target="tpu_custom_call" | custom-call | tf_op jit(solution)/shard_map/correlate/pallas_call | solution.py:289
  57.2 0.0 copy-start
  57.2 1.0 %copy-done = bf16[32,2,32,256]{3,2,1,0:T(8,128)(2,1)} copy-done((bf16[32,2,32,256]{3,2,1,0:T(8,128)(2,1)}, bf16[32,2,32,256]{3,2,1,0:T(8,128)(2,1)S(1)}, u32[]{:S(2)}) %copy-start) | copy-done | bytes 1048600
  58.2 2.9 %unscramble.1 = f32[2,16,64,256]{3,2,1,0:T(8,128)} custom-call(bf16[32,2,32,256]{3,2,1,0:T(8,128)(2,1)} %copy-done), custom_call_target="tpu_custom_call" | custom-call | tf_op jit(solution)/shard_map/unscramble/pallas_call | solution.py:321
  (1 shorter events, 0.0 us)
Async XLA Ops:
  0.0 3.6 %copy-start.1 = (bf16[8,256,256]{2,1,0:T(8,128)(2,1)S(1)}, bf16[8,256,256]{2,1,0:T(8,128)(2,1)}, u32[]{:S(2)}) copy-start(bf16[8,256,256]{2,1,0:T(8,128)(2,1)} %constant.10.clone.table) | copy-start | bytes 3145732
  57.2 1.0 %copy-start = (bf16[32,2,32,256]{3,2,1,0:T(8,128)(2,1)}, bf16[32,2,32,256]{3,2,1,0:T(8,128)(2,1)S(1)}, u32[]{:S(2)}) copy-start(bf16[32,2,32,256]{3,2,1,0:T(8,128)(2,1)S(1)} %correlate.1.recv) | copy-start | bytes 3145732

commit v3 on v2

v3 whole, which is shorter than its diff:
```python
import math

import jax
import jax.numpy as jnp
import numpy as np
from jax import lax
from jax.experimental import pallas as pl
from jax.experimental.pallas import tpu as pltpu
from jax.sharding import PartitionSpec as P

BINS = 8192
DEC = 8
OUT = 256
EPS = 1e-06
Q = 16
PERIOD = BINS // DEC
LANES = 128
SIDE = 4
ROWS = BINS // LANES
GROUP = 8
PATH = (
    ((0, 0), None),
    ((1, 0), (1, 0)),
    ((3, 0), (3, 0)),
    ((0, 1), (0, 1)),
    ((0, 3), (0, 3)),
    ((1, 1), (1, 0)),
    ((3, 3), (3, 0)),
    ((0, 2), (0, 1)),
    ((1, 3), (0, 3)),
    ((2, 0), (1, 0)),
    ((3, 1), (3, 0)),
    ((1, 2), (0, 1)),
    ((2, 1), (1, 0)),
    ((2, 3), (3, 0)),
    ((2, 2), (1, 0)),
    ((3, 2), (3, 0)),
)
ROUNDS = {1: range(1, 5), 4: range(5, 9), 7: range(9, 12), 10: range(12, 14), 13: range(14, 16)}


def lag_table():
    bins = np.arange(PERIOD)[:, None]
    lags = np.arange(OUT)[None, :] - OUT // 2
    angle = 2.0 * np.pi * ((bins * lags) % PERIOD) / PERIOD
    shape = (PERIOD // LANES, LANES, OUT)
    both = [np.cos(angle).reshape(shape), np.sin(angle).reshape(shape)]
    return (np.concatenate(both, axis=1) / math.sqrt(BINS)).astype(jnp.bfloat16)


def whiten(block, wide):
    values = block.astype(jnp.float32)
    total = jnp.sum(jnp.sum(values * values, axis=0, keepdims=True), axis=1, keepdims=True)
    wide[...] = values * lax.rsqrt(total / (2 * BINS) + EPS)
    return [wide[pl.ds(part, ROWS, stride=2), :].astype(jnp.bfloat16) for part in range(2)]


def find_slots(owner, found):
    stations = owner.shape[1]
    shape = (stations, stations)
    j = lax.broadcasted_iota(jnp.int32, shape, 0)
    b = lax.broadcasted_iota(jnp.int32, shape, 1)
    named = jnp.sum(jnp.where(j == b, owner[...], 0), axis=1, keepdims=True)
    hits = named == b
    first = jnp.min(jnp.where(hits, j, stations), axis=0, keepdims=True)
    last = jnp.max(jnp.where(hits, j, -1), axis=0, keepdims=True)
    found[0:1, 0:stations] = first
    found[1:2, 0:stations] = jnp.where(last > first, last, stations)


def fold(products):
    pairs = (products[0:16] + products[16:32]) + (products[32:48] + products[48:64])
    pairs = pairs.astype(jnp.float32)
    return pairs[0:8] + pairs[8:16]


def correlate(
    owner,
    x_in,
    s_in,
    table_in,
    recv,
    table,
    found,
    idx,
    wide,
    raw,
    xs,
    source,
    sb,
    ca,
    cb,
    stage,
    pair_send,
    pair_recv,
    local_sem,
    ring_send,
    ring_recv,
    out_send,
    out_recv,
    twin_send,
):
    blk = lax.axis_index("blk")
    band = lax.axis_index("band")
    blocks = SIDE**3
    stations = x_in.shape[0]
    twin = (blk, 1 - band)
    size_u = jnp.where(band == 0, SIDE, 1)
    size_r = jnp.where(band == 0, 1, SIDE)
    px, py, pv = blk % SIDE, (blk // SIDE) % SIDE, blk // (SIDE * SIDE)
    pr = jnp.where(band == 0, px, py)
    pu = jnp.where(band == 0, py, px)

    def number(v, u, r):
        return v * (SIDE * SIDE) + u * size_u + r * size_r

    def device(du, dv, dr):
        return (number((pv + dv) & 3, (pu + du) & 3, (pr + dr) & 3), band)

    def remote(src, dst, send, recv_sem, target):
        return pltpu.make_async_remote_copy(
            src_ref=src,
            dst_ref=dst,
            send_sem=send,
            recv_sem=recv_sem,
            device_id=target,
            device_id_type=pl.DeviceIdType.MESH,
        )

    barrier = pltpu.get_barrier_semaphore()
    greeted = [twin]
    for step in (1, 2, 3):
        greeted += [device(step, 0, 0), device(0, step, 0), device(0, 0, step)]
    greeted = [g for n, g in enumerate(greeted) if n not in (4, 5)]
    for target in greeted:
        pl.semaphore_signal(barrier, inc=1, device_id=target, device_id_type=pl.DeviceIdType.MESH)

    mine = pl.ds(pl.multiple_of(band * ROWS, ROWS), ROWS)
    source_keep = pltpu.make_async_copy(s_in.at[band], source.at[mine, :], local_sem.at[0])
    source_keep.start()
    station_keep = pltpu.make_async_copy(x_in, raw.at[:, mine, :], local_sem.at[1])
    station_keep.start()
    table_copy = pltpu.make_async_copy(table_in, table, local_sem.at[3])
    table_copy.start()
    find_slots(owner, found)
    index_copy = pltpu.make_async_copy(found, idx, local_sem.at[2])
    index_copy.start()
    xs[stations] = jnp.zeros(xs.shape[1:], xs.dtype)
    pl.semaphore_wait(barrier, len(greeted))

    source_out = remote(
        s_in.at[1 - band], source.at[mine, :], pair_send.at[0], pair_recv.at[0], twin
    )
    source_out.start()
    station_out = remote(x_in, raw.at[:, mine, :], pair_send.at[1], pair_recv.at[1], twin)
    station_out.start()
    source_keep.wait()
    source_out.wait_recv()
    own = whiten(source[...], wide.at[0])
    for part in range(2):
        sb[pv, pu, pr, part * ROWS : (part + 1) * ROWS] = own[part]
    pending = [source_out, station_out]

    def r_copy(step, at):
        block = sb.at[pv, pu, at]
        return remote(
            block, block, ring_send.at[15 + step - 1], ring_recv.at[15 + step - 1], device(0, 0, step)
        )

    for step in (1, 3, 2):
        copy = r_copy(step, pr)
        copy.start()
        pending.append(copy)
    for step in (1, 3, 2):
        r_copy(step, (pr + 4 - step) & 3).wait_recv()

    def row_copy(n, place):
        row = sb.at[(pv + 4 - place[1]) & 3, (pu + 4 - place[0]) & 3]
        step = PATH[n][1]
        return remote(
            row, row, ring_send.at[n - 1], ring_recv.at[n - 1], device(step[0], step[1], 0)
        )

    def pass_on(n):
        place = PATH[n][0]
        for child in range(1, 16):
            there, step = PATH[child]
            if ((there[0] - step[0]) % 4, (there[1] - step[1]) % 4) == place:
                row_copy(child, place).start()

    pass_on(0)
    index_copy.wait()
    table_copy.wait()

    station_keep.wait()
    station_out.wait_recv()

    @pl.loop(0, stations // 8)
    def _(group):
        for member in range(8):
            i = group * 8 + member
            real, imag = whiten(raw[i], wide.at[member])
            xs[i, 0] = real
            xs[i, 1] = imag
            xs[i, 2] = real + imag

    side = blk // (blocks // 2)
    row = blk % (blocks // 2)

    def block_at(turn):
        n, r = turn // SIDE, turn % SIDE
        du, dv = 0, 0
        for k in range(1, 16):
            (ku, kv), _ = PATH[k]
            du += jnp.where(n == k, ku, 0)
            dv += jnp.where(n == k, kv, 0)
        return (pv + 4 - dv) & 3, (pu + 4 - du) & 3, (pr + r) & 3

    @pl.loop(0, blocks // SIDE)
    def _(n):
        for when, arrivals in ROUNDS.items():

            @pl.when(n == when)
            def _():
                for k in arrivals:
                    row_copy(k, PATH[k][0]).wait_recv()
                    pass_on(k)

        @pl.loop(0, SIDE)
        def _(r):
            av, au, ar = block_at(n * SIDE + r)
            a = number(av, au, ar)
            real = sb[av, au, ar, pl.ds(0, ROWS), :]
            imag = sb[av, au, ar, pl.ds(ROWS, ROWS), :]
            less = real - imag
            more = real + imag
            base = ((n % 2) * SIDE + r) * (2 * Q * 8)
            for slot in range(2 * Q):
                i = idx[slot // Q, (a + blocks - slot % Q) & (blocks - 1)]
                k1 = fold(xs[i, 2] * imag)
                k2 = fold(xs[i, 0] * less)
                k3 = fold(xs[i, 1] * more)
                at = pl.ds(pl.multiple_of(base + slot * 8, 8), 8)
                ca[at, :] = k1 + k2
                cb[at, :] = k1 - k3

        @pl.when(n % 2 == 1)
        def _():
            lags = jnp.zeros((GROUP * 2 * Q, OUT), jnp.float32)
            for k in range(PERIOD // LANES):
                pick = pl.ds(k, GROUP * 2 * Q, stride=8)
                left = jnp.concatenate([ca[pick, :], cb[pick, :]], axis=1).astype(jnp.bfloat16)
                lags += jnp.dot(left, table[k], preferred_element_type=jnp.float32)
            first = (n // 2) * GROUP
            stage[pl.ds(first, GROUP)] = lags.astype(jnp.bfloat16).reshape(GROUP, 2 * Q, OUT)

            @pl.loop(0, GROUP)
            def _(member):
                turn = first + member
                av, au, ar = block_at(turn)

                @pl.when(turn > 0)
                def _():
                    remote(
                        stage.at[turn],
                        recv.at[row, band],
                        out_send,
                        out_recv,
                        (number(av, au, ar), side),
                    ).start()

    @pl.when(side == band)
    def _():
        pltpu.make_async_copy(stage.at[0], recv.at[row, band], out_recv).start()

    @pl.when(side != band)
    def _():
        copy = remote(stage.at[0], recv.at[row, band], twin_send, out_recv, twin)
        copy.start()
        copy.wait_send()

    for copy in pending:
        copy.wait_send()
    for n in range(1, 16):
        row_copy(n, PATH[n][0]).wait_send()
    pltpu.make_async_copy(
        stage.at[pl.ds(1, blocks - 1)], stage.at[pl.ds(1, blocks - 1)], out_send
    ).wait()
    pltpu.make_async_copy(recv, recv, out_recv).wait()


def unscramble(recv, out, near, wide, in_sem, out_sem):
    to = lax.broadcasted_iota(jnp.int32, (256, 256), 0)
    at = lax.broadcasted_iota(jnp.int32, (256, 256), 1)
    steps = [(s, g) for s in range(2) for g in range(4)]
    takes = []
    for n, (s, g) in enumerate(steps):
        block = pl.ds(8 * g, 8)
        take = pltpu.make_async_copy(recv.at[block, s], near.at[s, block], in_sem.at[n])
        take.start()
        takes.append(take)
    move = ((to % 16) * 16 + to // 16 == at).astype(jnp.bfloat16)
    gives = []
    for n, (s, g) in enumerate(steps):
        takes[n].wait()
        value = near[s, 8 * g : 8 * g + 8].reshape(256, OUT)
        value = jnp.dot(move, value, preferred_element_type=jnp.float32)
        wide[s, :, 16 * g : 16 * g + 16, :] = value.reshape(Q, 16, OUT)
        row = pl.ds(16 * g, 16)
        give = pltpu.make_async_copy(wide.at[s, :, row, :], out.at[s, :, row, :], out_sem.at[n])
        give.start()
        gives.append(give)
    for give in gives:
        give.wait()


def per_device(traces, sources, owner):
    stations = traces.shape[0]
    blocks = lax.axis_size("blk")
    tiles = traces.shape[2] // LANES
    x_in = traces.reshape(stations, 2, tiles, LANES).transpose(0, 2, 1, 3)
    x_in = x_in.reshape(stations, 2 * tiles, LANES)
    s_in = sources.reshape(2, 2, tiles, LANES).transpose(0, 2, 1, 3).reshape(2, 2 * tiles, LANES)
    table = jnp.asarray(lag_table())
    vmem = pl.BlockSpec(memory_space=pltpu.VMEM)
    recv = pl.pallas_call(
        correlate,
        out_shape=jax.ShapeDtypeStruct((blocks // 2, 2, 2 * Q, OUT), jnp.bfloat16),
        in_specs=[
            vmem,
            pl.BlockSpec(memory_space=pl.ANY),
            pl.BlockSpec(memory_space=pl.ANY),
            pl.BlockSpec(memory_space=pl.ANY),
        ],
        out_specs=pl.BlockSpec(memory_space=pl.ANY),
        scratch_shapes=[
            pltpu.VMEM((PERIOD // LANES, 2 * LANES, OUT), jnp.bfloat16),
            pltpu.VMEM((2, LANES), jnp.int32),
            pltpu.SMEM((2, LANES), jnp.int32),
            pltpu.VMEM((8, 2 * ROWS, LANES), jnp.float32),
            pltpu.VMEM((stations, 2 * ROWS, LANES), jnp.bfloat16),
            pltpu.VMEM((stations + 1, 3, ROWS, LANES), jnp.bfloat16),
            pltpu.VMEM((2 * ROWS, LANES), jnp.bfloat16),
            pltpu.VMEM((SIDE, SIDE, SIDE, 2 * ROWS, LANES), jnp.bfloat16),
            pltpu.VMEM((GROUP * 2 * Q * 8, LANES), jnp.float32),
            pltpu.VMEM((GROUP * 2 * Q * 8, LANES), jnp.float32),
            pltpu.VMEM((blocks, 2 * Q, OUT), jnp.bfloat16),
            pltpu.SemaphoreType.DMA((2,)),
            pltpu.SemaphoreType.DMA((2,)),
            pltpu.SemaphoreType.DMA((4,)),
            pltpu.SemaphoreType.DMA((18,)),
            pltpu.SemaphoreType.DMA((18,)),
            pltpu.SemaphoreType.DMA,
            pltpu.SemaphoreType.DMA,
            pltpu.SemaphoreType.DMA,
        ],
        compiler_params=pltpu.CompilerParams(
            has_side_effects=True, collective_id=0, vmem_limit_bytes=60 * 1024 * 1024
        ),
        name="correlate",
    )(owner.reshape(1, stations), x_in, s_in, table)
    return pl.pallas_call(
        unscramble,
        out_shape=jax.ShapeDtypeStruct((2, Q, 64, OUT), jnp.float32),
        in_specs=[pl.BlockSpec(memory_space=pl.ANY)],
        out_specs=pl.BlockSpec(memory_space=pl.ANY),
        scratch_shapes=[
            pltpu.VMEM((2, blocks // 2, 2 * Q, OUT), jnp.bfloat16),
            pltpu.VMEM((2, Q, 64, OUT), jnp.float32),
            pltpu.SemaphoreType.DMA((8,)),
            pltpu.SemaphoreType.DMA((8,)),
        ],
        compiler_params=pltpu.CompilerParams(vmem_limit_bytes=60 * 1024 * 1024),
        name="unscramble",
    )(recv)


def solution(mesh):
    placed = (P("blk", None, "band"), P("blk", None, "band"), P("blk", None))
    return jax.shard_map(
        per_device,
        mesh=mesh,
        in_specs=placed,
        out_specs=P("blk", None, "band", None),
        check_vma=False,
    )
```

time: 61.3 us -> 52.7 us (0.86)
  Pallas kernels: 56.5 us -> 52.6 us
  local copies, waits for them, and re-layouts: 3.63 us -> 0 us
  other arithmetic: 0.94 us -> 0 us
    pallas_call x1, Pallas kernels: 53.6 us -> 49.1 us  [per_device(): pl.pallas_call(correlate, out_shape=jax.ShapeDtypeStruct((blocks // 2, 2,...]
    reshape x2 -> x0, local copies, waits for them, and re-layouts: 2.65 us -> none  [the longest x1 1.85 us: per_device(): x_in = traces.reshape(stations, 2, ROWS // 2, LANES)]
    unnamed x4 -> x0, local copies, waits for them, and re-layouts: 0.99 us -> none
    reduce_min x1 -> x0, other arithmetic: 0.86 us -> none  [per_device(): first = jnp.min(jnp.where(hits, numbers, stations), axis=1)]
    pallas_call x1, Pallas kernels: 2.86 us -> 3.48 us  [per_device(): pl.pallas_call(unscramble, out_shape=jax.ShapeDtypeStruct((2, Q, 64, OUT)...]
where the time goes in v3:
time: 52.7 us; the launch traced here: 52.6 us
  Pallas kernels  52.6 us (100%)
    pallas_call x1, Pallas kernels, per_device(): pl.pallas_call(correlate, out_shape=jax.ShapeDtypeStruct((blocks // 2, 2,...  49.1 us
    pallas_call x1, Pallas kernels, per_device(): pl.pallas_call(unscramble, out_shape=jax.ShapeDtypeStruct((2, Q, 64, OUT)...  3.48 us

profile of v3, /device:TPU:1, one launch (start us, length us, event | category | flops | bytes accessed | tf_op | source)
XLA Modules:
  0.0 52.6 jit_solution(9879953324461566208)
XLA Ops:
  0.0 49.1 %correlate.1.recv = bf16[32,2,32,256]{3,2,1,0:T(8,128)(2,1)} custom-call(s32[1,64]{1,0:T(1,128)} %bitcast.13, bf16[64,64,128]{2,1,0:T(8,128)(2,1)} %bitcast.11, bf16[2,64,128]{2,1,0:T(8,128)(2,1)} %bitcast.12, bf16[8,256,256]{2,1,0:T(8,128)(2,1)} %constant.2.clone.table_in), custom_call_target="tpu_custom_call" | custom-call | tf_op jit(solution)/shard_map/correlate/pallas_call | solution.py:326
  49.1 3.5 %unscramble.1 = f32[2,16,64,256]{3,2,1,0:T(8,128)} custom-call(bf16[32,2,32,256]{3,2,1,0:T(8,128)(2,1)} %correlate.1.recv), custom_call_target="tpu_custom_call" | custom-call | tf_op jit(solution)/shard_map/unscramble/pallas_call | solution.py:362

commit v4 on v3

--- a/solution.py
+++ b/solution.py
@@ -36,7 +36,11 @@
     ((2, 2), (1, 0)),
     ((3, 2), (3, 0)),
 )
-ROUNDS = {1: range(1, 5), 4: range(5, 9), 7: range(9, 12), 10: range(12, 14), 13: range(14, 16)}
+CODES = [
+    np.uint32(sum((du + 4 * dv) << (4 * n) for n, ((du, dv), _) in enumerate(half))).astype(np.int32)
+    for half in (PATH[:8], PATH[8:])
+]
+ROUNDS = {1: range(1, 5), 5: range(5, 9), 9: range(9, 12), 12: range(12, 14), 14: range(14, 16)}
 
 
 def lag_table():
@@ -207,14 +211,36 @@
     side = blk // (blocks // 2)
     row = blk % (blocks // 2)
 
-    def block_at(turn):
-        n, r = turn // SIDE, turn % SIDE
-        du, dv = 0, 0
-        for k in range(1, 16):
-            (ku, kv), _ = PATH[k]
-            du += jnp.where(n == k, ku, 0)
-            dv += jnp.where(n == k, kv, 0)
-        return (pv + 4 - dv) & 3, (pu + 4 - du) & 3, (pr + r) & 3
+    def row_at(n):
+        code = jnp.where(n < 8, CODES[0], CODES[1]) >> ((n & 7) * 4)
+        return (pv + 4 - ((code >> 2) & 3)) & 3, (pu + 4 - (code & 3)) & 3
+
+    def send_lags(n, r):
+        v, u = row_at(n)
+        remote(
+            stage.at[n * SIDE + r],
+            recv.at[row, band],
+            out_send,
+            out_recv,
+            (number(v, u, (pr + r) & 3), side),
+        ).start()
+
+    def spectra(n, v, u, r):
+        ar = (pr + r) & 3
+        a = number(v, u, ar)
+        real = sb[v, u, ar, pl.ds(0, ROWS), :]
+        imag = sb[v, u, ar, pl.ds(ROWS, ROWS), :]
+        less = real - imag
+        more = real + imag
+        base = ((n % 2) * SIDE + r) * (2 * Q * 8)
+        for slot in range(2 * Q):
+            i = idx[slot // Q, (a + blocks - slot % Q) & (blocks - 1)]
+            k1 = fold(xs[i, 2] * imag)
+            k2 = fold(xs[i, 0] * less)
+            k3 = fold(xs[i, 1] * more)
+            at = pl.ds(pl.multiple_of(base + slot * 8, 8), 8)
+            ca[at, :] = k1 + k2
+            cb[at, :] = k1 - k3
 
     @pl.loop(0, blocks // SIDE)
     def _(n):
@@ -226,48 +252,34 @@
                     row_copy(k, PATH[k][0]).wait_recv()
                     pass_on(k)
 
+        @pl.when(n > 2)
+        def _():
+            send_lags(n - 2, 0)
+
+        @pl.when(n > 1)
+        def _():
+            for r in range(1, SIDE):
+                send_lags(n - 2, r)
+
+        v, u = row_at(n)
+
         @pl.loop(0, SIDE)
         def _(r):
-            av, au, ar = block_at(n * SIDE + r)
-            a = number(av, au, ar)
-            real = sb[av, au, ar, pl.ds(0, ROWS), :]
-            imag = sb[av, au, ar, pl.ds(ROWS, ROWS), :]
-            less = real - imag
-            more = real + imag
-            base = ((n % 2) * SIDE + r) * (2 * Q * 8)
-            for slot in range(2 * Q):
-                i = idx[slot // Q, (a + blocks - slot % Q) & (blocks - 1)]
-                k1 = fold(xs[i, 2] * imag)
-                k2 = fold(xs[i, 0] * less)
-                k3 = fold(xs[i, 1] * more)
-                at = pl.ds(pl.multiple_of(base + slot * 8, 8), 8)
-                ca[at, :] = k1 + k2
-                cb[at, :] = k1 - k3
+            spectra(n, v, u, r)
 
         @pl.when(n % 2 == 1)
         def _():
-            lags = jnp.zeros((GROUP * 2 * Q, OUT), jnp.float32)
+            total = jnp.zeros((GROUP * 2 * Q, OUT), jnp.float32)
             for k in range(PERIOD // LANES):
                 pick = pl.ds(k, GROUP * 2 * Q, stride=8)
                 left = jnp.concatenate([ca[pick, :], cb[pick, :]], axis=1).astype(jnp.bfloat16)
-                lags += jnp.dot(left, table[k], preferred_element_type=jnp.float32)
+                total += jnp.dot(left, table[k], preferred_element_type=jnp.float32)
             first = (n // 2) * GROUP
-            stage[pl.ds(first, GROUP)] = lags.astype(jnp.bfloat16).reshape(GROUP, 2 * Q, OUT)
-
-            @pl.loop(0, GROUP)
-            def _(member):
-                turn = first + member
-                av, au, ar = block_at(turn)
-
-                @pl.when(turn > 0)
-                def _():
-                    remote(
-                        stage.at[turn],
-                        recv.at[row, band],
-                        out_send,
-                        out_recv,
-                        (number(av, au, ar), side),
-                    ).start()
+            stage[pl.ds(first, GROUP)] = total.astype(jnp.bfloat16).reshape(GROUP, 2 * Q, OUT)
+
+    for n in (blocks // SIDE - 2, blocks // SIDE - 1):
+        for r in range(SIDE):
+            send_lags(n, r)
 
     @pl.when(side == band)
     def _():

time: 52.7 us -> 48.9 us (0.928)
  Pallas kernels: 52.6 us -> 48.8 us
    pallas_call x1, Pallas kernels: 49.1 us -> 45.3 us  [per_device(): pl.pallas_call(correlate, out_shape=jax.ShapeDtypeStruct((blocks // 2, 2,...]
where the time goes in v4:
time: 48.9 us; the launch traced here: 48.8 us
  Pallas kernels  48.8 us (100%)
    pallas_call x1, Pallas kernels, per_device(): pl.pallas_call(correlate, out_shape=jax.ShapeDtypeStruct((blocks // 2, 2,...  45.3 us
    pallas_call x1, Pallas kernels, per_device(): pl.pallas_call(unscramble, out_shape=jax.ShapeDtypeStruct((2, Q, 64, OUT)...  3.48 us

profile of v4, /device:TPU:1, one launch (start us, length us, event | category | flops | bytes accessed | tf_op | source)
XLA Modules:
  0.0 48.8 jit_solution(1364285009256469919)
XLA Ops:
  0.0 45.3 %correlate.1.recv = bf16[32,2,32,256]{3,2,1,0:T(8,128)(2,1)} custom-call(s32[1,64]{1,0:T(1,128)} %bitcast.13, bf16[64,64,128]{2,1,0:T(8,128)(2,1)} %bitcast.11, bf16[2,64,128]{2,1,0:T(8,128)(2,1)} %bitcast.12, bf16[8,256,256]{2,1,0:T(8,128)(2,1)} %constant.2.clone.table_in), custom_call_target="tpu_custom_call" | custom-call | tf_op jit(solution)/shard_map/correlate/pallas_call | solution.py:338
  45.3 3.5 %unscramble.1 = f32[2,16,64,256]{3,2,1,0:T(8,128)} custom-call(bf16[32,2,32,256]{3,2,1,0:T(8,128)(2,1)} %correlate.1.recv), custom_call_target="tpu_custom_call" | custom-call | tf_op jit(solution)/shard_map/unscramble/pallas_call | solution.py:374

commit v5 on v4

--- a/solution.py
+++ b/solution.py
@@ -36,11 +36,20 @@
     ((2, 2), (1, 0)),
     ((3, 2), (3, 0)),
 )
+WAVES = ((0,), (1, 2, 3, 4), (5, 6, 7, 8), (9, 10, 11), (12, 13), (14, 15))
+ORDER = [(k, part) for wave in WAVES for part in (0, 1) for k in wave]
+
+
+def word(values, bits):
+    return np.uint32(sum(int(v) << (bits * n) for n, v in enumerate(values))).astype(np.int32)
+
+
 CODES = [
-    np.uint32(sum((du + 4 * dv) << (4 * n) for n, ((du, dv), _) in enumerate(half))).astype(np.int32)
-    for half in (PATH[:8], PATH[8:])
+    word([PATH[k][0][0] + 4 * PATH[k][0][1] for k, _ in ORDER[n : n + 8]], 4) for n in (0, 8, 16, 24)
 ]
-ROUNDS = {1: range(1, 5), 5: range(5, 9), 9: range(9, 12), 12: range(12, 14), 14: range(14, 16)}
+HALVES = word([part for _, part in ORDER], 1)
+ROUNDS = {2: (1, 0), 6: (1, 1), 10: (2, 0), 14: (2, 1), 18: (3, 0), 21: (3, 1), 24: (4, 0), 26: (4, 1), 28: (5, 0), 30: (5, 1)}
+TAKES = sum(1 << when for when in ROUNDS)
 
 
 def lag_table():
@@ -168,7 +177,7 @@
     def r_copy(step, at):
         block = sb.at[pv, pu, at]
         return remote(
-            block, block, ring_send.at[15 + step - 1], ring_recv.at[15 + step - 1], device(0, 0, step)
+            block, block, ring_send.at[step - 1], ring_recv.at[step - 1], device(0, 0, step)
         )
 
     for step in (1, 3, 2):
@@ -178,21 +187,22 @@
     for step in (1, 3, 2):
         r_copy(step, (pr + 4 - step) & 3).wait_recv()
 
-    def row_copy(n, place):
-        row = sb.at[(pv + 4 - place[1]) & 3, (pu + 4 - place[0]) & 3]
+    def row_copy(n, part, place):
+        halves = pl.ds(part * 2, 2)
+        row = sb.at[(pv + 4 - place[1]) & 3, (pu + 4 - place[0]) & 3, halves]
         step = PATH[n][1]
-        return remote(
-            row, row, ring_send.at[n - 1], ring_recv.at[n - 1], device(step[0], step[1], 0)
-        )
-
-    def pass_on(n):
+        spot = 2 * n + part + 1
+        return remote(row, row, ring_send.at[spot], ring_recv.at[spot], device(step[0], step[1], 0))
+
+    def pass_on(n, part):
         place = PATH[n][0]
         for child in range(1, 16):
             there, step = PATH[child]
             if ((there[0] - step[0]) % 4, (there[1] - step[1]) % 4) == place:
-                row_copy(child, place).start()
-
-    pass_on(0)
+                row_copy(child, part, place).start()
+
+    for part in (0, 1):
+        pass_on(0, part)
     index_copy.wait()
     table_copy.wait()
 
@@ -211,28 +221,36 @@
     side = blk // (blocks // 2)
     row = blk % (blocks // 2)
 
-    def row_at(n):
-        code = jnp.where(n < 8, CODES[0], CODES[1]) >> ((n & 7) * 4)
-        return (pv + 4 - ((code >> 2) & 3)) & 3, (pu + 4 - (code & 3)) & 3
-
-    def send_lags(n, r):
-        v, u = row_at(n)
-        remote(
-            stage.at[n * SIDE + r],
-            recv.at[row, band],
-            out_send,
-            out_recv,
-            (number(v, u, (pr + r) & 3), side),
-        ).start()
-
-    def spectra(n, v, u, r):
-        ar = (pr + r) & 3
-        a = number(v, u, ar)
-        real = sb[v, u, ar, pl.ds(0, ROWS), :]
-        imag = sb[v, u, ar, pl.ds(ROWS, ROWS), :]
+    def half_row(n):
+        code = jnp.where(n < 8, CODES[0], CODES[1])
+        code = jnp.where(n < 16, code, jnp.where(n < 24, CODES[2], CODES[3])) >> ((n & 7) * 4)
+        return (pv + 4 - ((code >> 2) & 3)) & 3, (pu + 4 - (code & 3)) & 3, ((HALVES >> n) & 1) * 2
+
+    def send_lags(n, own_row):
+        v, u, first = half_row(n)
+        for j in range(2):
+
+            def send():
+                remote(
+                    stage.at[n * 2 + j],
+                    recv.at[row, band],
+                    out_send,
+                    out_recv,
+                    (number(v, u, first + j), side),
+                ).start()
+
+            if own_row:
+                pl.when(first + j != pr)(send)
+            else:
+                send()
+
+    def spectra(n, v, u, r, j):
+        a = number(v, u, r)
+        real = sb[v, u, r, pl.ds(0, ROWS), :]
+        imag = sb[v, u, r, pl.ds(ROWS, ROWS), :]
         less = real - imag
         more = real + imag
-        base = ((n % 2) * SIDE + r) * (2 * Q * 8)
+        base = ((n % 4) * 2 + j) * (2 * Q * 8)
         for slot in range(2 * Q):
             i = idx[slot // Q, (a + blocks - slot % Q) & (blocks - 1)]
             k1 = fold(xs[i, 2] * imag)
@@ -242,59 +260,62 @@
             ca[at, :] = k1 + k2
             cb[at, :] = k1 - k3
 
-    @pl.loop(0, blocks // SIDE)
+    steps = blocks // 2
+
+    @pl.loop(0, steps)
     def _(n):
-        for when, arrivals in ROUNDS.items():
-
-            @pl.when(n == when)
-            def _():
-                for k in arrivals:
-                    row_copy(k, PATH[k][0]).wait_recv()
-                    pass_on(k)
-
-        @pl.when(n > 2)
+        @pl.when(((TAKES >> n) & 1) == 1)
         def _():
-            send_lags(n - 2, 0)
-
-        @pl.when(n > 1)
+            for when, (wave, part) in ROUNDS.items():
+
+                @pl.when(n == when)
+                def _():
+                    for k in WAVES[wave]:
+                        row_copy(k, part, PATH[k][0]).wait_recv()
+                        pass_on(k, part)
+
+        @pl.when(n > 5)
         def _():
-            for r in range(1, SIDE):
-                send_lags(n - 2, r)
-
-        v, u = row_at(n)
-
-        @pl.loop(0, SIDE)
-        def _(r):
-            spectra(n, v, u, r)
-
-        @pl.when(n % 2 == 1)
+            send_lags(n - 4, False)
+
+        @pl.when((n == 4) | (n == 5))
+        def _():
+            send_lags(n - 4, True)
+
+        v, u, first = half_row(n)
+
+        @pl.loop(0, 2)
+        def _(j):
+            spectra(n, v, u, first + j, j)
+
+        @pl.when(n % 4 == 3)
         def _():
             total = jnp.zeros((GROUP * 2 * Q, OUT), jnp.float32)
             for k in range(PERIOD // LANES):
                 pick = pl.ds(k, GROUP * 2 * Q, stride=8)
                 left = jnp.concatenate([ca[pick, :], cb[pick, :]], axis=1).astype(jnp.bfloat16)
                 total += jnp.dot(left, table[k], preferred_element_type=jnp.float32)
-            first = (n // 2) * GROUP
-            stage[pl.ds(first, GROUP)] = total.astype(jnp.bfloat16).reshape(GROUP, 2 * Q, OUT)
-
-    for n in (blocks // SIDE - 2, blocks // SIDE - 1):
-        for r in range(SIDE):
-            send_lags(n, r)
+            at = (n // 4) * GROUP
+            stage[pl.ds(at, GROUP)] = total.astype(jnp.bfloat16).reshape(GROUP, 2 * Q, OUT)
+
+    for n in range(steps - 4, steps):
+        send_lags(n, False)
 
     @pl.when(side == band)
     def _():
-        pltpu.make_async_copy(stage.at[0], recv.at[row, band], out_recv).start()
+        pltpu.make_async_copy(stage.at[pr], recv.at[row, band], out_recv).start()
 
     @pl.when(side != band)
     def _():
-        copy = remote(stage.at[0], recv.at[row, band], twin_send, out_recv, twin)
+        copy = remote(stage.at[pr], recv.at[row, band], twin_send, out_recv, twin)
         copy.start()
         copy.wait_send()
 
     for copy in pending:
         copy.wait_send()
     for n in range(1, 16):
-        row_copy(n, PATH[n][0]).wait_send()
+        for part in (0, 1):
+            row_copy(n, part, PATH[n][0]).wait_send()
     pltpu.make_async_copy(
         stage.at[pl.ds(1, blocks - 1)], stage.at[pl.ds(1, blocks - 1)], out_send
     ).wait()
@@ -360,8 +381,8 @@
             pltpu.SemaphoreType.DMA((2,)),
             pltpu.SemaphoreType.DMA((2,)),
             pltpu.SemaphoreType.DMA((4,)),
-            pltpu.SemaphoreType.DMA((18,)),
-            pltpu.SemaphoreType.DMA((18,)),
+            pltpu.SemaphoreType.DMA((33,)),
+            pltpu.SemaphoreType.DMA((33,)),
             pltpu.SemaphoreType.DMA,
             pltpu.SemaphoreType.DMA,
             pltpu.SemaphoreType.DMA,

time: 48.9 us -> 48 us (0.982)
  Pallas kernels: 48.8 us -> 47.9 us
    pallas_call x1, Pallas kernels: 45.3 us -> 44.4 us  [per_device(): pl.pallas_call(correlate, out_shape=jax.ShapeDtypeStruct((blocks // 2, 2,...]
where the time goes in v5:
time: 48 us; the launch traced here: 47.9 us
  Pallas kernels  47.9 us (100%)
    pallas_call x1, Pallas kernels, per_device(): pl.pallas_call(correlate, out_shape=jax.ShapeDtypeStruct((blocks // 2, 2,...  44.4 us
    pallas_call x1, Pallas kernels, per_device(): pl.pallas_call(unscramble, out_shape=jax.ShapeDtypeStruct((2, Q, 64, OUT)...  3.48 us

profile of v5, /device:TPU:1, one launch (start us, length us, event | category | flops | bytes accessed | tf_op | source)
XLA Modules:
  0.0 47.9 jit_solution(2259294646060371229)
XLA Ops:
  0.0 44.4 %correlate.1.recv = bf16[32,2,32,256]{3,2,1,0:T(8,128)(2,1)} custom-call(s32[1,64]{1,0:T(1,128)} %bitcast.13, bf16[64,64,128]{2,1,0:T(8,128)(2,1)} %bitcast.11, bf16[2,64,128]{2,1,0:T(8,128)(2,1)} %bitcast.12, bf16[8,256,256]{2,1,0:T(8,128)(2,1)} %constant.2.clone.table_in), custom_call_target="tpu_custom_call" | custom-call | tf_op jit(solution)/shard_map/correlate/pallas_call | solution.py:359
  44.4 3.5 %unscramble.1 = f32[2,16,64,256]{3,2,1,0:T(8,128)} custom-call(bf16[32,2,32,256]{3,2,1,0:T(8,128)(2,1)} %correlate.1.recv), custom_call_target="tpu_custom_call" | custom-call | tf_op jit(solution)/shard_map/unscramble/pallas_call | solution.py:395

commit v6 on v5

--- a/solution.py
+++ b/solution.py
@@ -388,7 +388,7 @@
             pltpu.SemaphoreType.DMA,
         ],
         compiler_params=pltpu.CompilerParams(
-            has_side_effects=True, collective_id=0, vmem_limit_bytes=60 * 1024 * 1024
+            has_side_effects=True, collective_id=0, vmem_limit_bytes=52 * 1024 * 1024
         ),
         name="correlate",
     )(owner.reshape(1, stations), x_in, s_in, table)
@@ -403,7 +403,7 @@
             pltpu.SemaphoreType.DMA((8,)),
             pltpu.SemaphoreType.DMA((8,)),
         ],
-        compiler_params=pltpu.CompilerParams(vmem_limit_bytes=60 * 1024 * 1024),
+        compiler_params=pltpu.CompilerParams(vmem_limit_bytes=16 * 1024 * 1024),
         name="unscramble",
     )(recv)
 

time: 48 us -> 47.7 us (level)
  Pallas kernels: 47.9 us -> 46.1 us
  local copies, waits for them, and re-layouts: 0 us -> 1.41 us
    unnamed x0 -> x4, local copies, waits for them, and re-layouts: none -> 1.41 us
    pallas_call x1, Pallas kernels: 44.4 us -> 43.3 us  [per_device(): pl.pallas_call(correlate, out_shape=jax.ShapeDtypeStruct((blocks // 2, 2,...]
    pallas_call x1, Pallas kernels: 3.48 us -> 2.79 us  [per_device(): pl.pallas_call(unscramble, out_shape=jax.ShapeDtypeStruct((2, Q, 64, OUT)...]
where the time goes in v6:
time: 47.7 us; the launch traced here: 47.5 us
  Pallas kernels  46.1 us (97%)
  local copies, waits for them, and re-layouts  1.41 us (3%)
    pallas_call x1, Pallas kernels, per_device(): pl.pallas_call(correlate, out_shape=jax.ShapeDtypeStruct((blocks // 2, 2,...  43.3 us
    pallas_call x1, Pallas kernels, per_device(): pl.pallas_call(unscramble, out_shape=jax.ShapeDtypeStruct((2, Q, 64, OUT)...  2.79 us
    unnamed x4, local copies, waits for them, and re-layouts  1.41 us

profile of v6, /device:TPU:1, one launch (start us, length us, event | category | flops | bytes accessed | tf_op | source)
XLA Modules:
  0.0 47.5 jit_solution(1611634137784837223)
XLA Ops:
  0.0 0.0 copy-start
  0.0 0.8 %copy-done = bf16[2,2,4096]{2,1,0:T(2,128)(2,1)S(1)} copy-done((bf16[2,2,4096]{2,1,0:T(2,128)(2,1)S(1)}, bf16[2,2,4096]{2,1,0:T(2,128)(2,1)}, u32[]{:S(2)}) %copy-start) | copy-done | bytes 32792
  0.8 0.0 copy-start.1
  0.8 0.7 %copy-done.1 = s32[64,1]{0,1:T(1,128)S(1)} copy-done((s32[64,1]{0,1:T(1,128)S(1)}, s32[64,1]{0,1:T(1,128)}, u32[]{:S(2)}) %copy-start.1) | copy-done | bytes 280
  1.4 43.3 %correlate.1.recv = bf16[32,2,32,256]{3,2,1,0:T(8,128)(2,1)S(1)} custom-call(s32[1,64]{1,0:T(1,128)S(1)} %bitcast.12, bf16[64,64,128]{2,1,0:T(8,128)(2,1)} %bitcast.13, bf16[2,64,128]{2,1,0:T(8,128)(2,1)S(1)} %bitcast.11, bf16[8,256,256]{2,1,0:T(8,128)(2,1)} %constant.2.clone.table_in), custom_call_target="tpu_custom_call" | custom-call | tf_op jit(solution)/shard_map/correlate/pallas_call | solution.py:359
  44.8 2.8 %unscramble.1 = f32[2,16,64,256]{3,2,1,0:T(8,128)} custom-call(bf16[32,2,32,256]{3,2,1,0:T(8,128)(2,1)S(1)} %correlate.1.recv), custom_call_target="tpu_custom_call" | custom-call | tf_op jit(solution)/shard_map/unscramble/pallas_call | solution.py:395
Async XLA Ops:
  0.0 0.8 %copy-start = (bf16[2,2,4096]{2,1,0:T(2,128)(2,1)S(1)}, bf16[2,2,4096]{2,1,0:T(2,128)(2,1)}, u32[]{:S(2)}) copy-start(bf16[2,2,4096]{2,1,0:T(2,128)(2,1)} %param.5) | copy-start | bytes 98308
  0.8 0.7 %copy-start.1 = (s32[64,1]{0,1:T(1,128)S(1)}, s32[64,1]{0,1:T(1,128)}, u32[]{:S(2)}) copy-start(s32[64,1]{0,1:T(1,128)} %param.6) | copy-start | bytes 772
